TPU v7x, 256 devices: a whole 4x4x8 slice. The times are simulated.
256 devices in a mesh: lon: 32 (over z, x), lat: 2 (over core), head: 4 (over y).
Axes of the slice: x: 4, y: 4, z: 8, core: 2. Of those that a mesh axis runs over, the one named last changes fastest.
Arguments:
- queries: bfloat16 [32, 1280, 1024], P('lat', 'lon', 'head'), may hold values from -49 to 49
- keys: bfloat16 [32, 1280, 1024], P('lat', 'lon', 'head'), may hold values from -49 to 49
- values: bfloat16 [32, 1280, 1024], P('lat', 'lon', 'head'), may hold values from -16 to 16
- grad_out: bfloat16 [32, 1280, 1024], P('lat', 'lon', 'head'), may hold values from -64 to 64
- key_mask: int32 [32, 1280], P('lat', 'lon'), may hold values from 0 to 1
- offsets: int32 [4, 160], P('lat', 'lon'), may hold values from -8 to 8, as said below
- regions: int32 [4, 160], P('lat', 'lon'), may hold values from 0 to 7
Outputs:
- grad_queries: bfloat16 [32, 1280, 1024], P('lat', 'lon', 'head')
- grad_keys: bfloat16 [32, 1280, 1024], P('lat', 'lon', 'head')
- grad_values: bfloat16 [32, 1280, 1024], P('lat', 'lon', 'head')
Inputs may be any that keep to these rules, and one draw needn't show every extreme that they name: `offsets`: some block has offset -8 and some block has offset 8.
All inputs are finite; a program needn't handle non-finite values.
Results may differ from a plain program's by a relative error of at most 0.0095.
Values may be sent and summed in bfloat16 or wider, within the bound.
A program may use at most 64 MiB of HBM per device.

v0:
```python
import jax
import jax.numpy as jnp
from jax import lax
from jax.sharding import PartitionSpec as P

HS = 64
WIN = 8
REG_DEV = 8


MASKED_SCORE = -1e30


def extended_2(cells, sides, width):
    for axis, dim in sides:
        count = lax.axis_size(axis)
        head = lax.slice_in_dim(cells, 0, width, axis=dim)
        tail = lax.slice_in_dim(cells, cells.shape[dim] - width, cells.shape[dim], axis=dim)
        cells = jnp.concatenate(
            [
                lax.ppermute(tail, axis, [(i, (i + 1) % count) for i in range(count)]),
                cells,
                lax.ppermute(head, axis, [((i + 1) % count, i) for i in range(count)]),
            ],
            axis=dim,
        )
    return cells


def split_heads(array, head_count):
    return array.reshape(array.shape[:-1] + (head_count, HS))


def to_blocks(array):
    lat_cells, lon_cells = (array.shape[0], array.shape[1])
    trailing = array.shape[2:]
    grid_blocks = array.reshape((lat_cells // WIN, WIN, lon_cells // WIN, WIN) + trailing)
    perm_axes = (0, 2, 1, 3) + tuple(range(4, grid_blocks.ndim))
    return grid_blocks.transpose(perm_axes).reshape(
        (lat_cells // WIN, lon_cells // WIN, WIN * WIN) + trailing
    )


def from_blocks(array):
    lat_blocks, lon_blocks = (array.shape[0], array.shape[1])
    trailing = array.shape[3:]
    grid_blocks = array.reshape((lat_blocks, lon_blocks, WIN, WIN) + trailing)
    perm_axes = (0, 2, 1, 3) + tuple(range(4, grid_blocks.ndim))
    return grid_blocks.transpose(perm_axes).reshape((lat_blocks * WIN, lon_blocks * WIN) + trailing)


def window_blocks(extended, along):
    lon_blocks = extended.shape[1] - 4
    return jnp.concatenate([extended[:, step : step + lon_blocks] for step in range(5)], axis=along)


def fold_blocks(grads):
    cells = WIN * WIN
    folded = None
    for step in range(5):
        piece = grads[:, :, step * cells : (step + 1) * cells]
        piece = jnp.pad(piece, ((0, 0), (step, 4 - step), (0, 0), (0, 0)))
        folded = piece if folded is None else folded + piece
    return folded


def local(queries, keys, values, grad_out, key_mask, offsets, regions):
    highest = lax.Precision.HIGHEST
    lat_cells, lon_cells, features = queries.shape
    head_count = features // HS
    logit_scale = HS ** (-0.5)
    rim_blocks = 2
    cell_count = lat_cells * lon_cells
    lat_blocks, lon_blocks = (lat_cells // WIN, lon_cells // WIN)
    key_blocks = to_blocks(keys)
    value_blocks = to_blocks(values)
    query_blocks = to_blocks(queries)
    cotan_blocks = to_blocks(grad_out)
    mask_blocks = to_blocks(key_mask)
    block_region = jnp.broadcast_to(
        regions[:, :, None], (lat_blocks, lon_blocks, WIN * WIN)
    ).reshape(cell_count)
    weights = (block_region[:, None] == jnp.arange(REG_DEV, dtype=jnp.int32)[None, :]).astype(
        jnp.float32
    )
    weights = weights * mask_blocks.reshape(cell_count).astype(jnp.float32)[:, None]
    divisor = jnp.maximum(jnp.sum(weights, axis=0), 1.0)
    weights_low = weights.astype(jnp.bfloat16).T
    pooled_k = jnp.dot(
        weights_low, key_blocks.reshape(cell_count, features), preferred_element_type=jnp.float32
    )
    pooled_v = jnp.dot(
        weights_low, value_blocks.reshape(cell_count, features), preferred_element_type=jnp.float32
    )
    pooled = (jnp.stack([pooled_k, pooled_v], axis=1) / divisor[:, None, None]).astype(jnp.bfloat16)
    gathered = lax.all_gather(pooled, "lat", axis=0, tiled=True)
    reg_count = gathered.shape[0]
    register_key_rows = gathered[:, 0].reshape(reg_count, head_count, HS)
    register_value_rows = gathered[:, 1].reshape(reg_count, head_count, HS)
    key_ext, value_ext, mask_ext = (
        extended_2(key_blocks, (("lon", 1),), rim_blocks),
        extended_2(value_blocks, (("lon", 1),), rim_blocks),
        extended_2(mask_blocks, (("lon", 1),), rim_blocks),
    )
    cand_k = split_heads(window_blocks(key_ext, 2), head_count)
    candidate_values = split_heads(window_blocks(value_ext, 2), head_count)
    cand_mask = window_blocks(mask_ext, 2)
    key_offset = (
        jnp.arange(5, dtype=jnp.int32)[:, None, None] * WIN
        - 2 * WIN
        + jnp.zeros((1, WIN, 1), jnp.int32)
        + jnp.arange(WIN, dtype=jnp.int32)[None, None, :]
    ).reshape(5 * WIN * WIN)
    window_start = offsets[:, :, None]
    usable = (
        (key_offset >= window_start - WIN)
        & (key_offset < window_start + 2 * WIN)
        & (cand_mask == 1)
    )
    usable_b = usable[:, :, None, None, :]
    query_block = split_heads(query_blocks, head_count)
    gradient_block = split_heads(cotan_blocks, head_count)
    score_win = (
        jnp.einsum("abqhd,abkhd->abhqk", query_block, cand_k, preferred_element_type=jnp.float32)
        * logit_scale
    )
    score_win = jnp.where(usable_b, score_win, MASKED_SCORE)
    register_scores = (
        jnp.einsum(
            "abqhd,khd->abhqk", query_block, register_key_rows, preferred_element_type=jnp.float32
        )
        * logit_scale
    )
    row_max = jnp.maximum(jnp.max(score_win, axis=-1), jnp.max(register_scores, axis=-1))
    exp_total = jnp.sum(jnp.where(usable_b, jnp.exp(score_win - row_max[..., None]), 0.0), axis=-1)
    exp_total = exp_total + jnp.sum(jnp.exp(register_scores - row_max[..., None]), axis=-1)
    log_total = row_max + jnp.log(exp_total)
    prob_win = jnp.where(usable_b, jnp.exp(score_win - log_total[..., None]), 0.0)
    prob_reg = jnp.exp(register_scores - log_total[..., None])
    window_lower_bound = prob_win.astype(jnp.bfloat16)
    register_lower_bound = prob_reg.astype(jnp.bfloat16)
    attended_output = jnp.einsum(
        "abhqk,abkhd->abqhd",
        window_lower_bound,
        candidate_values,
        preferred_element_type=jnp.float32,
    )
    attended_output = attended_output + jnp.einsum(
        "abhqk,khd->abqhd",
        register_lower_bound,
        register_value_rows,
        preferred_element_type=jnp.float32,
    )
    delta_dot = jnp.sum(gradient_block.astype(jnp.float32) * attended_output, axis=-1)
    delta_heads = delta_dot.transpose(0, 1, 3, 2)
    dprob_win = jnp.einsum(
        "abqhd,abkhd->abhqk", gradient_block, candidate_values, preferred_element_type=jnp.float32
    )
    register_prob_gradient = jnp.einsum(
        "abqhd,khd->abhqk", gradient_block, register_value_rows, preferred_element_type=jnp.float32
    )
    dscore_win = (prob_win * (dprob_win - delta_heads[..., None])).astype(jnp.bfloat16)
    register_score_gradient = (prob_reg * (register_prob_gradient - delta_heads[..., None])).astype(
        jnp.bfloat16
    )
    grad_q = logit_scale * (
        jnp.einsum("abhqk,abkhd->abqhd", dscore_win, cand_k, preferred_element_type=jnp.float32)
        + jnp.einsum(
            "abhqk,khd->abqhd",
            register_score_gradient,
            register_key_rows,
            preferred_element_type=jnp.float32,
        )
    )
    grad_queries = from_blocks(grad_q.reshape(lat_blocks, lon_blocks, WIN * WIN, features)).astype(
        jnp.bfloat16
    )
    reg_grad_k = logit_scale * jnp.einsum(
        "abhqk,abqhd->khd", register_score_gradient, query_block, preferred_element_type=jnp.float32
    )
    reg_grad_v = jnp.einsum(
        "abhqk,abqhd->khd", register_lower_bound, gradient_block, preferred_element_type=jnp.float32
    )
    reg_grads = jnp.stack(
        [reg_grad_k.reshape(reg_count, features), reg_grad_v.reshape(reg_count, features)], axis=1
    )
    own_grads = lax.psum_scatter(
        reg_grads.astype(jnp.bfloat16), "lat", scatter_dimension=0, tiled=True
    ).astype(jnp.float32)
    spread = jnp.dot(
        weights,
        (own_grads / divisor[:, None, None]).reshape(REG_DEV, 2 * features),
        precision=highest,
    )
    spread = spread.reshape(lat_blocks, lon_blocks, WIN * WIN, 2 * features)
    grad_kc = logit_scale * jnp.einsum(
        "abhqk,abqhd->abkhd", dscore_win, query_block, preferred_element_type=jnp.float32
    )
    grad_vc = jnp.einsum(
        "abhqk,abqhd->abkhd", window_lower_bound, gradient_block, preferred_element_type=jnp.float32
    )
    ext_k = fold_blocks(grad_kc.reshape(grad_kc.shape[:3] + (features,)))
    ext_v = fold_blocks(grad_vc.reshape(grad_vc.shape[:3] + (features,)))
    edges_k = jnp.concatenate([ext_k[:, :rim_blocks], ext_k[:, -rim_blocks:]], axis=1)
    edges_v = jnp.concatenate([ext_v[:, :rim_blocks], ext_v[:, -rim_blocks:]], axis=1)
    got_k, got_v = (
        extended_2(edges_k, (("lon", 1),), rim_blocks),
        extended_2(edges_v, (("lon", 1),), rim_blocks),
    )
    win_k = ext_k[:, rim_blocks:-rim_blocks].at[:, :rim_blocks].add(got_k[:, :rim_blocks])
    win_k = win_k.at[:, -rim_blocks:].add(got_k[:, -rim_blocks:])
    win_v = ext_v[:, rim_blocks:-rim_blocks].at[:, :rim_blocks].add(got_v[:, :rim_blocks])
    win_v = win_v.at[:, -rim_blocks:].add(got_v[:, -rim_blocks:])
    grad_keys = from_blocks((win_k + spread[..., :features]).astype(jnp.bfloat16))
    grad_values = from_blocks((win_v + spread[..., features:]).astype(jnp.bfloat16))
    return (grad_queries, grad_keys, grad_values)


def solution(mesh):
    in_specs = (
        P("lat", "lon", "head"),
        P("lat", "lon", "head"),
        P("lat", "lon", "head"),
        P("lat", "lon", "head"),
        P("lat", "lon"),
        P("lat", "lon"),
        P("lat", "lon"),
    )
    out_specs = (P("lat", "lon", "head"), P("lat", "lon", "head"), P("lat", "lon", "head"))
    return jax.shard_map(local, mesh=mesh, in_specs=in_specs, out_specs=out_specs, check_vma=False)
```

profile of v0, /device:TPU:1, one launch (start us, length us, event | category | flops | bytes accessed | tf_op | source)
XLA Modules:
  0.0 155.2 jit_solution(9662106261121816254)
XLA Ops:
  8.1 2.1 %collective-permute-start.2 = (s32[2,2,64]{2,0,1:T(2,128)S(1)}, s32[2,2,64]{2,0,1:T(2,128)S(1)}, u32[]{:S(2)}, u32[]{:S(2)}) collective-permute-start(s32[2,2,64]{2,0,1:T(2,128)S(1)} %get-tuple-element.97), channel_id=1, source_target_pairs={{0,8},{8,16},{16,24},{24,32},{32,40},{40,48},{48,56},{56,64},{64,7... | collective-permute-start | bytes 3080 | tf_op jit(solution)/shard_map/ppermute | solution.py:21
  10.3 6.6 %collective-permute-start.3 = (s32[2,2,64]{2,0,1:T(2,128)S(1)}, s32[2,2,64]{2,0,1:T(2,128)S(1)}, u32[]{:S(2)}, u32[]{:S(2)}) collective-permute-start(s32[2,2,64]{2,0,1:T(2,128)S(1)} %get-tuple-element.96), channel_id=1, source_target_pairs={{8,0},{16,8},{24,16},{32,24},{40,32},{48,40},{56,48},{64,56},{72,6... | collective-permute-start | bytes 3080 | tf_op jit(solution)/shard_map/ppermute | solution.py:23
  21.8 4.7 %collective-permute-start.5 = (bf16[2,2,64,256]{3,2,1,0:T(8,128)(2,1)}, bf16[2,2,64,256]{3,2,1,0:T(8,128)(2,1)}, u32[]{:S(2)}, u32[]{:S(2)}) collective-permute-start(bf16[2,2,64,256]{3,2,1,0:T(8,128)(2,1)} %get-tuple-element.77), channel_id=1, source_target_pairs={{8,0},{16,8},{24,16},{32,24},{40,32},{48,40},{56,48},{64,56},{72,6... | collective-permute-start | bytes 393224 | tf_op jit(solution)/shard_map/ppermute | solution.py:23
  27.6 3.6 %all_gather.3 = bf16[16,2,256]{2,0,1:T(8,128)(2,1)S(1)} all-gather(bf16[8,2,256]{2,0,1:T(8,128)(2,1)S(1)} %fusion.51), channel_id=1, replica_groups=mesh['lon'=32,'lat'=2,'head'=4] {'lat'}, dimensions={0}, use_global_device_ids=true | all-gather | bytes 24576 | tf_op jit(solution)/shard_map/all_gather | solution.py:96
  44.7 4.1 %concatenate.77 = bf16[2,5,320,4,64]{2,4,3,1,0:T(8,128)(2,1)S(1)} concatenate(bf16[2,5,64,4,64]{2,4,3,1,0:T(8,128)(2,1)} %bitcast.189, bf16[2,5,64,4,64]{2,4,3,1,0:T(8,128)(2,1)} %bitcast.191, bf16[2,5,64,4,64]{2,4,3,1,0:T(8,128)(2,1)} %copy.410, bf16[2,5,64,4,64]{2,4,3,1,0:T(8,128)(2,1)} %bitcast.193, bf16[2,5,64,4,64]{2,4,3,1,0:T(8,128)(2,1)} %bitcast.195), dimensions={2} | concatenate | bytes 3276800 | tf_op jit(solution)/shard_map/concatenate | solution.py:54
  48.8 1.9 %bitcast_reduce_fusion = (f32[2,5,4,64]{3,2,1,0:T(4,128)S(1)}, f32[2,5,4,320,64]{3,4,2,1,0:T(8,128)S(1)}) fusion(pred[2,5,320]{2,1,0:T(8,128)(4,1)S(1)} %copy.416, bf16[2,5,64,4,64]{2,4,3,1,0:T(8,128)(2,1)} %copy.447, bf16[2,5,320,4,64]{2,4,3,1,0:T(8,128)(2,1)S(1)} %concatenate.77), kind=kOutput, calls=%fused_computation.4 | convolution fusion | flops 107312640 | bytes 5256320 | tf_op jit(solution)/shard_map/abqhd,abkhd->abhqk/dot_general | solution.py:124
  52.8 2.1 %pad_maximum_fusion = (bf16[2,5,64,256]{3,2,1,0:T(8,128)(2,1)}, bf16[2,5,64,256]{3,2,1,0:T(8,128)(2,1)}, bf16[2,5,64,256]{3,2,1,0:T(8,128)(2,1)}, bf16[2,5,64,256]{3,2,1,0:T(8,128)(2,1)}) fusion(bf16[2,2,64,256]{3,2,1,0:T(8,128)(2,1)} %collective-permute-done.5, bf16[2,5,64,256]{3,2,1,0:T(8,128)(2,1)S(1)} %bitcast.184, ...), kind=kLoop, calls=%fused_computation.62 | loop fusion | flops 655360 | bytes 1900544 | tf_op jit(solution)/shard_map/concatenate | solution.py:19
  54.9 2.2 %copy.428 = bf16[2,5,64,256]{2,3,1,0:T(8,128)(2,1)} copy(bf16[2,5,64,256]{3,2,1,0:T(8,128)(2,1)} %get-tuple-element.75) | data formatting | bytes 655360 | tf_op jit(solution)/shard_map/slice | solution.py:54
  57.0 2.0 %copy.429 = bf16[2,5,64,256]{2,3,1,0:T(8,128)(2,1)} copy(bf16[2,5,64,256]{3,2,1,0:T(8,128)(2,1)} %get-tuple-element.76) | data formatting | bytes 655360 | tf_op jit(solution)/shard_map/slice | solution.py:54
  59.1 2.1 %copy.431 = bf16[2,5,64,256]{2,3,1,0:T(8,128)(2,1)} copy(bf16[2,5,64,256]{3,2,1,0:T(8,128)(2,1)} %get-tuple-element.68) | data formatting | bytes 655360 | tf_op jit(solution)/shard_map/slice | solution.py:54
  63.7 5.3 %concatenate.88 = bf16[2,5,320,4,64]{2,4,3,1,0:T(8,128)(2,1)} concatenate(bf16[2,5,64,4,64]{2,4,3,1,0:T(8,128)(2,1)} %bitcast.188, bf16[2,5,64,4,64]{2,4,3,1,0:T(8,128)(2,1)} %bitcast.190, bf16[2,5,64,4,64]{2,4,3,1,0:T(8,128)(2,1)} %copy.433, bf16[2,5,64,4,64]{2,4,3,1,0:T(8,128)(2,1)} %bitcast.192, bf16[2,5,64,4,64]{2,4,3,1,0:T(8,128)(2,1)} %bitcast.194), dimensions={2} | concatenate | bytes 3276800 | tf_op jit(solution)/shard_map/concatenate | solution.py:54
  69.0 4.5 %fusion.12 = f32[2,5,64,4]{2,3,1,0:T(4,128)S(1)} fusion(f32[2,5,64,4,64]{2,4,3,1,0:T(8,128)} %convolution_bitcast_fusion.3, bf16[2,5,320,4,64]{2,4,3,1,0:T(8,128)(2,1)} %concatenate.88, bf16[2,5,64,4,64]{2,4,3,1,0:T(8,128)(2,1)S(1)} %copy-done.27, f32[2,5,4,320,64]{3,4,2,1,0:T(8,128)} %copy-done, f32[2,5,4,64]{3,2,1,0:T(4,128)S(1)} %fusion.47, ...), kind=kOutput, calls=%fused_computation.22 | convolution fusion | flops 109606400 | bytes 5921920 | tf_op jit(solution)/shard_map/abhqk,abkhd->abqhd/dot_general | solution.py:142
  73.9 2.7 %fusion = bf16[2,5,4,64,320]{4,3,2,1,0:T(8,128)(2,1)} fusion(f32[2,5,4,320,64]{3,4,2,1,0:T(8,128)S(1)} %copy-done.1, bf16[2,5,64,4,64]{2,4,3,1,0:T(8,128)(2,1)S(1)} %copy-done.27, bf16[2,5,320,4,64]{2,4,3,1,0:T(8,128)(2,1)S(1)} %copy-done.28, f32[2,5,4,64]{3,2,1,0:T(4,128)S(1)} %bitcast.214, f32[2,5,4,64]{3,2,1,0:T(4,128)S(1)} %fusion.47, ...), kind=kOutput, calls=%fused_computation.1 | convolution fusion | flops 110592000 | bytes 6904960 | tf_op jit(solution)/shard_map/abqhd,abkhd->abhqk/dot_general | solution.py:156
  77.9 3.6 %fusion.68 = (f32[2,5,64,256]{2,3,1,0:T(8,128)}, f32[2,5,64,256]{2,3,1,0:T(8,128)}, f32[2,5,64,256]{2,3,1,0:T(8,128)}, f32[2,5,64,256]{2,3,1,0:T(8,128)}, f32[2,5,64,256]{2,3,1,0:T(8,128)}) fusion(f32[2,5,320,256]{2,3,1,0:T(8,128)S(1)} %bitcast.181), kind=kLoop, calls=%fused_computation.132 | loop fusion | bytes 6553600 | tf_op jit(solution)/shard_map/slice | solution.py:61
  81.5 1.7 %copy.497 = f32[2,5,64,256]{3,2,1,0:T(8,128)S(1)} copy(f32[2,5,64,256]{2,3,1,0:T(8,128)} %get-tuple-element.55) | data formatting | bytes 1310720
  83.2 2.5 %copy.496 = f32[2,5,64,256]{3,2,1,0:T(8,128)} copy(f32[2,5,64,256]{2,3,1,0:T(8,128)} %get-tuple-element.52) | data formatting | bytes 1310720
  85.8 2.6 %copy.495 = f32[2,5,64,256]{3,2,1,0:T(8,128)} copy(f32[2,5,64,256]{2,3,1,0:T(8,128)} %get-tuple-element.53) | data formatting | bytes 1310720
  88.3 2.6 %copy.494 = f32[2,5,64,256]{3,2,1,0:T(8,128)} copy(f32[2,5,64,256]{2,3,1,0:T(8,128)} %get-tuple-element.54) | data formatting | bytes 1310720
  90.9 2.5 %copy.493 = f32[2,5,64,256]{3,2,1,0:T(8,128)} copy(f32[2,5,64,256]{2,3,1,0:T(8,128)} %get-tuple-element.51) | data formatting | bytes 1310720
  93.5 3.1 %pad_add_fusion = f32[2,9,64,256]{3,2,1,0:T(8,128)} fusion(f32[2,5,64,256]{3,2,1,0:T(8,128)S(1)} %copy.497, f32[2,5,64,256]{3,2,1,0:T(8,128)} %copy.496, f32[2,5,64,256]{3,2,1,0:T(8,128)} %copy.495, f32[2,5,64,256]{3,2,1,0:T(8,128)} %copy.494, f32[2,5,64,256]{3,2,1,0:T(8,128)} %copy.493), kind=kLoop, calls=%fused_computation.28 | loop fusion | flops 1179648 | bytes 4456448 | tf_op jit(solution)/shard_map/add | solution.py:63
  99.6 2.5 %convolution_multiply_fusion = f32[2,5,4,320,64]{3,4,2,1,0:T(8,128)} fusion(bf16[2,5,64,4,64]{2,4,3,1,0:T(8,128)(2,1)S(1)} %copy-done.23, bf16[2,5,4,64,320]{4,3,2,1,0:T(8,128)(2,1)S(1)} %copy-done.22), kind=kOutput, calls=%fused_computation.12 | convolution fusion | flops 105676800 | bytes 5242880 | tf_op jit(solution)/shard_map/abhqk,abqhd->abkhd/dot_general | solution.py:196
  104.6 6.2 %fusion.69 = (f32[2,5,64,256]{2,3,1,0:T(8,128)}, f32[2,5,64,256]{2,3,1,0:T(8,128)S(1)}, f32[2,5,64,256]{2,3,1,0:T(8,128)}, f32[2,5,64,256]{2,3,1,0:T(8,128)}, f32[2,5,64,256]{2,3,1,0:T(8,128)}) fusion(f32[2,5,320,256]{2,3,1,0:T(8,128)} %bitcast.180), kind=kLoop, calls=%fused_computation.133 | loop fusion | bytes 6553600 | tf_op jit(solution)/shard_map/slice | solution.py:61
  110.8 1.7 %copy.492 = f32[2,5,64,256]{3,2,1,0:T(8,128)S(1)} copy(f32[2,5,64,256]{2,3,1,0:T(8,128)} %get-tuple-element.60) | data formatting | bytes 1310720
  112.9 1.9 %copy.490 = f32[2,5,64,256]{3,2,1,0:T(8,128)S(1)} copy(f32[2,5,64,256]{2,3,1,0:T(8,128)} %get-tuple-element.58) | data formatting | bytes 1310720
  114.8 1.9 %copy.489 = f32[2,5,64,256]{3,2,1,0:T(8,128)S(1)} copy(f32[2,5,64,256]{2,3,1,0:T(8,128)} %get-tuple-element.59) | data formatting | bytes 1310720
  116.8 2.8 %copy.488 = f32[2,5,64,256]{3,2,1,0:T(8,128)} copy(f32[2,5,64,256]{2,3,1,0:T(8,128)} %get-tuple-element.56) | data formatting | bytes 1310720
  119.6 2.4 %pad_add_fusion.1 = f32[2,9,64,256]{3,2,1,0:T(8,128)} fusion(f32[2,5,64,256]{3,2,1,0:T(8,128)S(1)} %copy.492, f32[2,5,64,256]{3,2,1,0:T(8,128)S(1)} %copy.491, f32[2,5,64,256]{3,2,1,0:T(8,128)S(1)} %copy.490, f32[2,5,64,256]{3,2,1,0:T(8,128)S(1)} %copy.489, f32[2,5,64,256]{3,2,1,0:T(8,128)} %copy.488), kind=kLoop, calls=%fused_computation.29 | loop fusion | flops 1179648 | bytes 4456448 | tf_op jit(solution)/shard_map/add | solution.py:63
  125.5 2.1 %slice.319 = f32[2,5,64,256]{3,2,1,0:T(8,128)} slice(f32[2,9,64,256]{3,2,1,0:T(8,128)} %pad_add_fusion), slice={[0:2], [2:7], [0:64], [0:256]} | slice | bytes 1310720 | tf_op jit(solution)/shard_map/slice | solution.py:212
  127.6 4.8 %collective-permute-start.9 = (f32[2,2,64,256]{3,2,1,0:T(8,128)}, f32[2,2,64,256]{3,2,1,0:T(8,128)S(1)}, u32[]{:S(2)}, u32[]{:S(2)}) collective-permute-start(f32[2,2,64,256]{3,2,1,0:T(8,128)} %get-tuple-element.61), channel_id=1, source_target_pairs={{8,0},{16,8},{24,16},{32,24},{40,32},{48,40},{56,48},{64,56},{72,6... | collective-permute-start | bytes 786440 | tf_op jit(solution)/shard_map/ppermute | solution.py:23
  132.4 4.8 %collective-permute-start.7 = (f32[2,2,64,256]{3,2,1,0:T(8,128)}, f32[2,2,64,256]{3,2,1,0:T(8,128)}, u32[]{:S(2)}, u32[]{:S(2)}) collective-permute-start(f32[2,2,64,256]{3,2,1,0:T(8,128)} %get-tuple-element.63), channel_id=1, source_target_pairs={{8,0},{16,8},{24,16},{32,24},{40,32},{48,40},{56,48},{64,56},{72,6... | collective-permute-start | bytes 786440 | tf_op jit(solution)/shard_map/ppermute | solution.py:23
  139.5 1.9 %fusion.36 = f32[2,5,64,256]{3,2,1,0:T(8,128)} fusion(f32[2,5,64,256]{3,2,1,0:T(8,128)} %slice.319, f32[2,2,64,256]{3,2,1,0:T(8,128)} %collective-permute-done.8, f32[2,5,64,256]{3,2,1,0:T(8,128)S(1)} %copy.497, f32[2,5,64,256]{3,2,1,0:T(8,128)S(1)} %copy-done.3, f32[2,5,64,256]{3,2,1,0:T(8,128)S(1)} %copy-done.5, f32[2,5,64,256]{3,2,1,0:T(8,128)S(1)} %copy-done.7, ...), kind=kLoop, calls=%fused_computation.76 | loop fusion | flops 327680 | bytes 3801088 | tf_op jit(solution)/shard_map/scatter-add | solution.py:212
  141.4 3.1 %collective-permute-done.6 = f32[2,2,64,256]{3,2,1,0:T(8,128)} collective-permute-done((f32[2,2,64,256]{3,2,1,0:T(8,128)}, f32[2,2,64,256]{3,2,1,0:T(8,128)}, u32[]{:S(2)}, u32[]{:S(2)}) %collective-permute-start.6) | collective-permute-done | bytes 262176 | tf_op jit(solution)/shard_map/ppermute | solution.py:21
  (171 shorter events, 41.8 us)
Async XLA Ops:
  7.2 19.3 %copy-start.30 = (bf16[16,40,256]{2,1,0:T(8,128)(2,1)S(1)}, bf16[16,40,256]{2,1,0:T(8,128)(2,1)}, u32[]{:S(2)}) copy-start(bf16[16,40,256]{2,1,0:T(8,128)(2,1)} %param.15) | copy-start | bytes 983044
  7.2 130.0 %reduce-scatter.4.cloned.1.call-start = ((), (), s32[]{:S(2)}) async-start(), calls=%async_computation.1 | async-start | bytes 24576
  8.1 30.8 %collective-permute-start.2 = (s32[2,2,64]{2,0,1:T(2,128)S(1)}, s32[2,2,64]{2,0,1:T(2,128)S(1)}, u32[]{:S(2)}, u32[]{:S(2)}) collective-permute-start(s32[2,2,64]{2,0,1:T(2,128)S(1)} %get-tuple-element.97), channel_id=1, source_target_pairs={{0,8},{8,16},{16,24},{24,32},{32,40},{40,48},{48,56},{56,64},{64,7... | collective-permute-start | bytes 3080 | tf_op jit(solution)/shard_map/ppermute | solution.py:21
  10.3 28.7 %collective-permute-start.3 = (s32[2,2,64]{2,0,1:T(2,128)S(1)}, s32[2,2,64]{2,0,1:T(2,128)S(1)}, u32[]{:S(2)}, u32[]{:S(2)}) collective-permute-start(s32[2,2,64]{2,0,1:T(2,128)S(1)} %get-tuple-element.96), channel_id=1, source_target_pairs={{8,0},{16,8},{24,16},{32,24},{40,32},{48,40},{56,48},{64,56},{72,6... | collective-permute-start | bytes 3080 | tf_op jit(solution)/shard_map/ppermute | solution.py:23
  16.9 10.0 %copy-start.31 = (s32[2,5]{1,0:T(2,128)S(1)}, s32[2,5]{1,0:T(2,128)}, u32[]{:S(2)}) copy-start(s32[2,5]{1,0:T(2,128)} %param.21) | copy-start | bytes 124
  18.6 20.6 %collective-permute-start.1 = (bf16[2,2,64,256]{3,2,1,0:T(8,128)(2,1)}, bf16[2,2,64,256]{3,2,1,0:T(8,128)(2,1)}, u32[]{:S(2)}, u32[]{:S(2)}) collective-permute-start(bf16[2,2,64,256]{3,2,1,0:T(8,128)(2,1)} %get-tuple-element.83), channel_id=1, source_target_pairs={{8,0},{16,8},{24,16},{32,24},{40,32},{48,40},{56,48},{64,56},{72,6... | collective-permute-start | bytes 393224 | tf_op jit(solution)/shard_map/ppermute | solution.py:23
  20.0 19.2 %collective-permute-start = (bf16[2,2,64,256]{3,2,1,0:T(8,128)(2,1)}, bf16[2,2,64,256]{3,2,1,0:T(8,128)(2,1)}, u32[]{:S(2)}, u32[]{:S(2)}) collective-permute-start(bf16[2,2,64,256]{3,2,1,0:T(8,128)(2,1)} %get-tuple-element.84), channel_id=1, source_target_pairs={{0,8},{8,16},{16,24},{24,32},{32,40},{40,48},{48,56},{56,64},{64,7... | collective-permute-start | bytes 393224 | tf_op jit(solution)/shard_map/ppermute | solution.py:21
  21.8 10.2 %copy-start.32 = (s32[2,5]{1,0:T(2,128)S(1)}, s32[2,5]{1,0:T(2,128)}, u32[]{:S(2)}) copy-start(s32[2,5]{1,0:T(2,128)} %param.20) | copy-start | bytes 124
  21.8 31.0 %collective-permute-start.5 = (bf16[2,2,64,256]{3,2,1,0:T(8,128)(2,1)}, bf16[2,2,64,256]{3,2,1,0:T(8,128)(2,1)}, u32[]{:S(2)}, u32[]{:S(2)}) collective-permute-start(bf16[2,2,64,256]{3,2,1,0:T(8,128)(2,1)} %get-tuple-element.77), channel_id=1, source_target_pairs={{8,0},{16,8},{24,16},{32,24},{40,32},{48,40},{56,48},{64,56},{72,6... | collective-permute-start | bytes 393224 | tf_op jit(solution)/shard_map/ppermute | solution.py:23
  26.8 6.6 %copy-start.24 = (bf16[2,5,64,4,64]{4,3,2,1,0:T(4,128)(2,1)}, bf16[2,5,64,4,64]{4,3,2,1,0:T(4,128)(2,1)S(1)}, u32[]{:S(2)}) copy-start(bf16[2,5,64,4,64]{4,3,2,1,0:T(4,128)(2,1)S(1)} %reshape_reshape.14) | copy-start | bytes 983044
  32.0 30.3 %copy-start.20 = (f32[2,5,4,64,16]{3,4,1,0,2:T(8,128)}, f32[2,5,4,64,16]{3,4,1,0,2:T(8,128)S(1)}, u32[]{:S(2)}) copy-start(f32[2,5,4,64,16]{3,4,1,0,2:T(8,128)S(1)} %get-tuple-element.103) | copy-start | bytes 491524
  38.9 13.9 %collective-permute-start.4 = (bf16[2,2,64,256]{3,2,1,0:T(8,128)(2,1)S(1)}, bf16[2,2,64,256]{3,2,1,0:T(8,128)(2,1)}, u32[]{:S(2)}, u32[]{:S(2)}) collective-permute-start(bf16[2,2,64,256]{3,2,1,0:T(8,128)(2,1)S(1)} %get-tuple-element.78), channel_id=1, source_target_pairs={{0,8},{8,16},{16,24},{24,32},{32,40},{40,48},{48,56},{56,64},{64,7... | collective-permute-start | bytes 393224 | tf_op jit(solution)/shard_map/ppermute | solution.py:21
  54.9 6.3 %copy-start.29 = (bf16[2,5,64,256]{3,2,1,0:T(8,128)(2,1)S(1)}, bf16[2,5,64,256]{3,2,1,0:T(8,128)(2,1)}, u32[]{:S(2)}) copy-start(bf16[2,5,64,256]{3,2,1,0:T(8,128)(2,1)} %get-tuple-element.67) | copy-start | bytes 983044
  63.7 5.3 %copy-start.27 = (bf16[2,5,64,4,64]{2,4,3,1,0:T(8,128)(2,1)S(1)}, bf16[2,5,64,4,64]{2,4,3,1,0:T(8,128)(2,1)}, u32[]{:S(2)}) copy-start(bf16[2,5,64,4,64]{2,4,3,1,0:T(8,128)(2,1)} %copy.436) | copy-start | bytes 983044
  112.5 9.5 %copy-start.10 = (f32[2,5,64,256]{3,2,1,0:T(8,128)}, f32[2,5,64,256]{3,2,1,0:T(8,128)S(1)}, u32[]{:S(2)}) copy-start(f32[2,5,64,256]{3,2,1,0:T(8,128)S(1)} %copy.492) | copy-start | bytes 1966084
  112.9 9.1 %copy-start.12 = (f32[2,5,64,256]{3,2,1,0:T(8,128)}, f32[2,5,64,256]{3,2,1,0:T(8,128)S(1)}, u32[]{:S(2)}) copy-start(f32[2,5,64,256]{3,2,1,0:T(8,128)S(1)} %copy.491) | copy-start | bytes 1966084
  114.8 7.2 %copy-start.14 = (f32[2,5,64,256]{3,2,1,0:T(8,128)}, f32[2,5,64,256]{3,2,1,0:T(8,128)S(1)}, u32[]{:S(2)}) copy-start(f32[2,5,64,256]{3,2,1,0:T(8,128)S(1)} %copy.490) | copy-start | bytes 1966084
  116.8 5.2 %copy-start.16 = (f32[2,5,64,256]{3,2,1,0:T(8,128)}, f32[2,5,64,256]{3,2,1,0:T(8,128)S(1)}, u32[]{:S(2)}) copy-start(f32[2,5,64,256]{3,2,1,0:T(8,128)S(1)} %copy.489) | copy-start | bytes 1966084
  125.5 14.0 %copy-start.3 = (f32[2,5,64,256]{3,2,1,0:T(8,128)S(1)}, f32[2,5,64,256]{3,2,1,0:T(8,128)}, u32[]{:S(2)}) copy-start(f32[2,5,64,256]{3,2,1,0:T(8,128)} %copy.496) | copy-start | bytes 1966084
  125.5 14.0 %copy-start.5 = (f32[2,5,64,256]{3,2,1,0:T(8,128)S(1)}, f32[2,5,64,256]{3,2,1,0:T(8,128)}, u32[]{:S(2)}) copy-start(f32[2,5,64,256]{3,2,1,0:T(8,128)} %copy.495) | copy-start | bytes 1966084
  125.5 14.0 %copy-start.7 = (f32[2,5,64,256]{3,2,1,0:T(8,128)S(1)}, f32[2,5,64,256]{3,2,1,0:T(8,128)}, u32[]{:S(2)}) copy-start(f32[2,5,64,256]{3,2,1,0:T(8,128)} %copy.494) | copy-start | bytes 1966084
  125.5 14.0 %copy-start.9 = (f32[2,5,64,256]{3,2,1,0:T(8,128)S(1)}, f32[2,5,64,256]{3,2,1,0:T(8,128)}, u32[]{:S(2)}) copy-start(f32[2,5,64,256]{3,2,1,0:T(8,128)} %copy.493) | copy-start | bytes 1966084
  127.6 11.8 %collective-permute-start.8 = (f32[2,2,64,256]{3,2,1,0:T(8,128)}, f32[2,2,64,256]{3,2,1,0:T(8,128)}, u32[]{:S(2)}, u32[]{:S(2)}) collective-permute-start(f32[2,2,64,256]{3,2,1,0:T(8,128)} %get-tuple-element.62), channel_id=1, source_target_pairs={{0,8},{8,16},{16,24},{24,32},{32,40},{40,48},{48,56},{56,64},{64,7... | collective-permute-start | bytes 786440 | tf_op jit(solution)/shard_map/ppermute | solution.py:21
  127.6 17.9 %collective-permute-start.9 = (f32[2,2,64,256]{3,2,1,0:T(8,128)}, f32[2,2,64,256]{3,2,1,0:T(8,128)S(1)}, u32[]{:S(2)}, u32[]{:S(2)}) collective-permute-start(f32[2,2,64,256]{3,2,1,0:T(8,128)} %get-tuple-element.61), channel_id=1, source_target_pairs={{8,0},{16,8},{24,16},{32,24},{40,32},{48,40},{56,48},{64,56},{72,6... | collective-permute-start | bytes 786440 | tf_op jit(solution)/shard_map/ppermute | solution.py:23
  132.4 12.0 %collective-permute-start.6 = (f32[2,2,64,256]{3,2,1,0:T(8,128)}, f32[2,2,64,256]{3,2,1,0:T(8,128)}, u32[]{:S(2)}, u32[]{:S(2)}) collective-permute-start(f32[2,2,64,256]{3,2,1,0:T(8,128)} %get-tuple-element.64), channel_id=1, source_target_pairs={{0,8},{8,16},{16,24},{24,32},{32,40},{40,48},{48,56},{56,64},{64,7... | collective-permute-start | bytes 786440 | tf_op jit(solution)/shard_map/ppermute | solution.py:21
  132.4 13.2 %collective-permute-start.7 = (f32[2,2,64,256]{3,2,1,0:T(8,128)}, f32[2,2,64,256]{3,2,1,0:T(8,128)}, u32[]{:S(2)}, u32[]{:S(2)}) collective-permute-start(f32[2,2,64,256]{3,2,1,0:T(8,128)} %get-tuple-element.63), channel_id=1, source_target_pairs={{8,0},{16,8},{24,16},{32,24},{40,32},{48,40},{56,48},{64,56},{72,6... | collective-permute-start | bytes 786440 | tf_op jit(solution)/shard_map/ppermute | solution.py:23
  138.0 6.5 %slice-start = ((f32[2,9,64,256]{3,2,1,0:T(8,128)}), f32[2,5,64,256]{3,2,1,0:T(8,128)S(1)}, s32[]{:S(2)}) async-start(f32[2,9,64,256]{3,2,1,0:T(8,128)} %pad_add_fusion.1), calls=%async_computation.2 | async-start | bytes 1310720 | tf_op jit(solution)/shard_map/slice | solution.py:210
  139.4 5.1 %copy-start.11 = (f32[2,5,64,256]{3,2,1,0:T(8,128)S(1)}, f32[2,5,64,256]{3,2,1,0:T(8,128)}, u32[]{:S(2)}) copy-start(f32[2,5,64,256]{3,2,1,0:T(8,128)} %copy-done.10) | copy-start | bytes 1966084
  139.4 5.1 %copy-start.13 = (f32[2,5,64,256]{3,2,1,0:T(8,128)S(1)}, f32[2,5,64,256]{3,2,1,0:T(8,128)}, u32[]{:S(2)}) copy-start(f32[2,5,64,256]{3,2,1,0:T(8,128)} %copy-done.12) | copy-start | bytes 1966084
  139.4 5.1 %copy-start.15 = (f32[2,5,64,256]{3,2,1,0:T(8,128)S(1)}, f32[2,5,64,256]{3,2,1,0:T(8,128)}, u32[]{:S(2)}) copy-start(f32[2,5,64,256]{3,2,1,0:T(8,128)} %copy-done.14) | copy-start | bytes 1966084
  139.4 5.1 %copy-start.17 = (f32[2,5,64,256]{3,2,1,0:T(8,128)S(1)}, f32[2,5,64,256]{3,2,1,0:T(8,128)}, u32[]{:S(2)}) copy-start(f32[2,5,64,256]{3,2,1,0:T(8,128)} %copy-done.16) | copy-start | bytes 1966084
  139.4 5.1 %copy-start.19 = (f32[2,5,64,256]{3,2,1,0:T(8,128)S(1)}, f32[2,5,64,256]{3,2,1,0:T(8,128)}, u32[]{:S(2)}) copy-start(f32[2,5,64,256]{3,2,1,0:T(8,128)} %copy.488) | copy-start | bytes 1966084
  (13 other events, 36.0 us)
Sparse Core Ops, SparseCore 0:
  104.7 11.7 reduce-scatter.3
where the time goes:
time: 156 us; the launch traced here: 155 us
  local copies, waits for them, and re-layouts  72 us (46%)
  starting transfers between devices  24.5 us (16%)
  matrix products  20 us (13%)
  other arithmetic  17.2 us (11%)
  between operations  14.7 us (9%)
  blocking collectives  3.59 us (2%)
  waiting for transfers between devices  3.11 us (2%)
    unnamed x78, local copies, waits for them, and re-layouts  22.7 us
    ppermute x5, starting transfers between devices, extended_2(): lax.ppermute(head, axis, [((i + 1) % count, i) for i in range(count)])  22.3 us
    concatenate x7, local copies, waits for them, and re-layouts, window_blocks(): jnp.concatenate([extended[:, step:step + lon_blocks] for step in range(5)...  12.5 us
    slice x10, local copies, waits for them, and re-layouts, window_blocks(): extended[:, step:step + lon_blocks]  11.8 us
    slice x2, local copies, waits for them, and re-layouts, fold_blocks(): piece = grads[:, :, step * cells:(step + 1) * cells]  9.79 us
    add x2, other arithmetic, fold_blocks(): folded = piece if folded is None else folded + piece  5.51 us
    dot_general x1, matrix products, local(): jnp.einsum('abhqk,abkhd->abqhd', window_lower_bound, candidate_values, pr...  4.53 us
    all_gather x1, blocking collectives, local(): gathered = lax.all_gather(pooled, 'lat', axis=0, tiled=True)  3.59 us
  transfers between devices with their start and end apart: 11, of which 1 were waited for; matrix products, arithmetic and copies ran while one was open for 34% of the time, Pallas kernels for 0%

commit v1 on v0

v1 whole, which is shorter than its diff:
```python
import jax
import jax.numpy as jnp
from jax import lax
from jax.experimental import pallas as pl
from jax.experimental.pallas import tpu as pltpu
from jax.sharding import PartitionSpec as P

HS = 64
WIN = 8
CELLS = WIN * WIN
REG_DEV = 8
NA = 2
NB = 5
MASKED = -1.0e30
FLOOR = -1.0e29
SCALE = HS ** (-0.5)
MESH = pl.DeviceIdType.MESH
NT = (((1,), (1,)), ((), ()))
TN = (((0,), (0,)), ((), ()))
F32 = jnp.float32
BF16 = jnp.bfloat16

EDGE = ((0, 0, 3), (1, 0, 4), (3, 1, 5), (4, 2, 5))
FOREIGN = ((0, 0, -2, 0, 1), (0, 1, -1, 0, 2), (1, 0, 5, 3, 5), (1, 1, 6, 4, 5))


def dot(a, b, dims=(((1,), (0,)), ((), ()))):
    return lax.dot_general(a, b, dims, preferred_element_type=F32)


def kernel(
    q_hbm, k_hbm, v_hbm, g_hbm, mask_hbm, off_hbm, reg_hbm,
    o_q, o_k, o_v,
    q_in, k_in, v_in, g_in, kb, vb, mrep,
    fq, fg, e_s, p_s, dk_s, dv_s, dq_s, rk_s, rv_s,
    pool, rsend, rrecv, st_out, st_in, pst_out, pst_in, dq_out, dq_in,
    mask_ref, off_ref, reg_ref,
    in_sem, qg_ss, qg_rs, st_ss, st_rs, pst_ss, pst_rs, dq_ss, dq_rs, lat_ss, lat_rs,
):
    count = lax.axis_size("lon")
    me = lax.axis_index("lon")
    right = lax.rem(me + 1, count)
    left = lax.rem(me + count - 1, count)
    peer = 1 - lax.axis_index("lat")
    sides = ({"lon": left}, {"lon": right})

    barrier = pltpu.get_barrier_semaphore()
    for device in sides + ({"lat": peer},):
        pl.semaphore_signal(barrier, inc=1, device_id=device, device_id_type=MESH)
    loads = [
        pltpu.make_async_copy(src, dst, in_sem.at[i])
        for i, (src, dst) in enumerate((
            (mask_hbm, mask_ref), (off_hbm, off_ref), (reg_hbm, reg_ref),
            (k_hbm, k_in), (v_hbm, v_in), (q_hbm, q_in), (g_hbm, g_in),
        ))
    ]
    for copy in loads:
        copy.start()
    pl.semaphore_wait(barrier, 3)

    def qg_copy(side, a, slot, kind):
        block = slot + (0 if side == 0 else 3)
        src = (q_hbm, g_hbm)[kind]
        dst = (fq, fg)[kind]
        return pltpu.make_async_remote_copy(
            src.at[a, :, block], dst.at[1 - side, a, slot],
            qg_ss.at[side, a, slot, kind], qg_rs.at[1 - side, a, slot, kind],
            device_id=sides[side], device_id_type=MESH,
        )

    for a in range(NA):
        for slot in range(2):
            for kind in range(2):
                for side in range(2):
                    qg_copy(side, a, slot, kind).start()

    def rows_copy(src, dst, ss, rs, side, a):
        return pltpu.make_async_remote_copy(
            src.at[side, a], dst.at[1 - side, a], ss.at[side, a], rs.at[1 - side, a],
            device_id=sides[side], device_id_type=MESH,
        )

    lane_head = lax.broadcasted_iota(jnp.int32, (CELLS, 4 * HS), 1) // HS
    head_mask = [(lane_head == h).astype(F32).astype(BF16) for h in range(4)]
    low_half = lax.broadcasted_iota(jnp.int32, (CELLS, 128), 1) < HS

    def block_diag(x):
        return jnp.concatenate([x * head_mask[h] for h in range(4)], axis=0)

    def diag_rows(full):
        return jnp.concatenate(
            [
                jnp.where(low_half, full[0:64, 0:128], full[64:128, 0:128]),
                jnp.where(low_half, full[128:192, 128:256], full[192:256, 128:256]),
            ],
            axis=1,
        )

    for copy in loads:
        copy.wait()

    cell_t = lax.broadcasted_iota(jnp.int32, (CELLS, NB * WIN), 0) % WIN
    lane = lax.broadcasted_iota(jnp.int32, (CELLS, NB * WIN), 1)
    row8 = lax.broadcasted_iota(jnp.int32, (REG_DEV, 256), 0)
    pk = jnp.zeros((REG_DEV, 256), F32)
    pv = jnp.zeros((REG_DEV, 256), F32)
    cnt = jnp.zeros((REG_DEV, 256), F32)
    for a in range(NA):
        mask8 = mask_ref[a * WIN : (a + 1) * WIN, :].astype(F32)
        mask64 = jnp.broadcast_to(mask8[:, None, :], (WIN, WIN, NB * WIN)).reshape(CELLS, NB * WIN)
        for b in range(NB):
            column = jnp.sum(jnp.where(lane == cell_t + b * WIN, mask64, 0.0), axis=1, keepdims=True)
            rep = jnp.broadcast_to(column, (CELLS, 128))
            mrep[a, b * CELLS : (b + 1) * CELLS, :] = rep
            rep2 = jnp.concatenate([rep, rep], axis=1)
            kx = k_in[a, :, b].reshape(CELLS, 256)
            vx = v_in[a, :, b].reshape(CELLS, 256)
            kb[a, b * CELLS : (b + 1) * CELLS, :] = kx
            vb[a, b * CELLS : (b + 1) * CELLS, :] = vx
            mine = row8 == reg_ref[a, b]
            pk = pk + jnp.where(mine, jnp.sum(kx.astype(F32) * rep2, axis=0, keepdims=True), 0.0)
            pv = pv + jnp.where(mine, jnp.sum(vx.astype(F32) * rep2, axis=0, keepdims=True), 0.0)
            cnt = cnt + jnp.where(mine, jnp.sum(rep2, axis=0, keepdims=True), 0.0)
    divisor = jnp.maximum(cnt, 1.0)
    pool[0, 0] = (pk / divisor).astype(BF16)
    pool[0, 1] = (pv / divisor).astype(BF16)
    pool_copy = pltpu.make_async_remote_copy(
        pool.at[0], pool.at[1], lat_ss.at[0], lat_rs.at[0], device_id={"lat": peer}, device_id_type=MESH
    )
    pool_copy.start()
    dk_s[...] = jnp.zeros_like(dk_s)
    dv_s[...] = jnp.zeros_like(dv_s)
    rk_s[...] = jnp.zeros_like(rk_s)
    rv_s[...] = jnp.zeros_like(rv_s)
    pool_copy.wait_recv()
    reg_k = jnp.concatenate([pool[0, 0].astype(F32), pool[1, 0].astype(F32)], axis=0).astype(BF16)
    reg_v = jnp.concatenate([pool[0, 1].astype(F32), pool[1, 1].astype(F32)], axis=0).astype(BF16)

    def bias(a, block, first, end, start):
        rows = (end - first) * CELLS
        row = lax.broadcasted_iota(jnp.int32, (rows, 128), 0)
        key_off = row // CELLS * WIN + row % WIN + (first - block) * WIN
        usable = (key_off >= start - WIN) & (key_off < start + 2 * WIN)
        usable = usable & (mrep[a, first * CELLS : end * CELLS, :] > 0.5)
        half = jnp.where(usable, 0.0, MASKED)
        return jnp.concatenate([half, half], axis=1)

    def partial_stats(keys, values, bdq, bdg, add):
        s = dot(keys, bdq, NT) + add
        dp = dot(values, bdg, NT)
        top = jnp.maximum(jnp.max(s, axis=0, keepdims=True), FLOOR)
        e = jnp.exp(s - top)
        total = jnp.sum(e, axis=0, keepdims=True)
        inner = jnp.sum(e * dp, axis=0, keepdims=True)
        return e, dp, (top, total, inner)

    def merged(x, y):
        top = jnp.maximum(x[0], y[0])
        fx = jnp.exp(x[0] - top)
        fy = jnp.exp(y[0] - top)
        inverse = 1.0 / (x[1] * fx + y[1] * fy)
        return fx * inverse, (x[2] * fx + y[2] * fy) * inverse

    def grads(a, first, end, keys, bdq, bdg, e, dp, alpha, delta, regs):
        rows = (end - first) * CELLS
        p = e * alpha
        ds = (p * (dp - delta)).astype(BF16)
        p = p.astype(BF16)
        dv = dot(p, bdg)
        dk = dot(ds, bdq)
        dv_s[a, first * CELLS : end * CELLS, :] += dv[:rows]
        dk_s[a, first * CELLS : end * CELLS, :] += dk[:rows]
        if regs:
            rv_s[...] += dv[rows:]
            rk_s[...] += dk[rows:]
        return diag_rows(dot(ds, keys, TN)) * SCALE

    def local_q(a, block):
        bdq = block_diag(q_in[a, :, block].reshape(CELLS, 256) * jnp.asarray(SCALE, BF16))
        bdg = block_diag(g_in[a, :, block].reshape(CELLS, 256))
        return bdq, bdg

    def local_keys(a, first, end):
        keys = jnp.concatenate([kb[a, first * CELLS : end * CELLS, :], reg_k], axis=0)
        values = jnp.concatenate([vb[a, first * CELLS : end * CELLS, :], reg_v], axis=0)
        return keys, values

    def local_stats(a, block, first, end):
        keys, values = local_keys(a, first, end)
        bdq, bdg = local_q(a, block)
        add = jnp.concatenate(
            [bias(a, block, first, end, off_ref[a, block]), jnp.zeros((2 * REG_DEV, 256), F32)], axis=0
        )
        e, dp, stats = partial_stats(keys, values, bdq, bdg, add)
        return keys, bdq, bdg, e, dp, stats

    def edge_stats(a, carry):
        for i, (block, first, end) in enumerate(EDGE):
            rows = (end - first) * CELLS + 2 * REG_DEV
            _, _, _, e, dp, stats = local_stats(a, block, first, end)
            e_s[a, i, :rows] = e
            p_s[a, i, :rows] = dp
            side, slot = i // 2, i % 2
            st_out[side, a, slot, 0:1] = stats[0]
            st_out[side, a, slot, 1:2] = stats[1]
            st_out[side, a, slot, 2:3] = stats[2]
            st_out[side, a, slot, 3:4] = jnp.full((1, 256), off_ref[a, block], jnp.int32).astype(F32)
        for side in range(2):
            rows_copy(st_out, st_in, st_ss, st_rs, side, a).start()
        return carry

    def middle(a, carry):
        keys, bdq, bdg, e, dp, stats = local_stats(a, 2, 0, NB)
        inverse = 1.0 / stats[1]
        dq = grads(a, 0, NB, keys, bdq, bdg, e, dp, inverse, stats[2] * inverse, True)
        o_q[a, :, 2] = dq.reshape(WIN, WIN, 256).astype(BF16)
        return carry

    def foreign(a, carry):
        for side in range(2):
            for slot in range(2):
                for kind in range(2):
                    qg_copy(1 - side, a, slot, kind).wait_recv()
            rows_copy(st_out, st_in, st_ss, st_rs, 1 - side, a).wait_recv()
        for side, slot, block, first, end in FOREIGN:
            keys = kb[a, first * CELLS : end * CELLS, :]
            values = vb[a, first * CELLS : end * CELLS, :]
            bdq = block_diag(fq[side, a, slot].reshape(CELLS, 256) * jnp.asarray(SCALE, BF16))
            bdg = block_diag(fg[side, a, slot].reshape(CELLS, 256))
            theirs = tuple(st_in[side, a, slot, r : r + 1] for r in range(3))
            start = st_in[side, a, slot, 3:4, 0:128].astype(jnp.int32)
            e, dp, stats = partial_stats(keys, values, bdq, bdg, bias(a, block, first, end, start))
            for r in range(3):
                pst_out[side, a, slot, r : r + 1] = stats[r]
            alpha, delta = merged(stats, theirs)
            dq = grads(a, first, end, keys, bdq, bdg, e, dp, alpha, delta, False)
            dq_out[side, a, slot] = dq.astype(BF16)
        for side in range(2):
            rows_copy(pst_out, pst_in, pst_ss, pst_rs, side, a).start()
            rows_copy(dq_out, dq_in, dq_ss, dq_rs, side, a).start()
        return carry

    def finish(a, carry):
        for side in range(2):
            rows_copy(pst_out, pst_in, pst_ss, pst_rs, 1 - side, a).wait_recv()
        for i, (block, first, end) in enumerate(EDGE):
            side, slot = i // 2, i % 2
            rows = (end - first) * CELLS + 2 * REG_DEV
            keys, _ = local_keys(a, first, end)
            bdq, bdg = local_q(a, block)
            mine = tuple(st_out[side, a, slot, r : r + 1] for r in range(3))
            theirs = tuple(pst_in[side, a, slot, r : r + 1] for r in range(3))
            alpha, delta = merged(mine, theirs)
            dq_s[a, i] = grads(
                a, first, end, keys, bdq, bdg, e_s[a, i, :rows], p_s[a, i, :rows], alpha, delta, True
            )
        return carry

    lax.fori_loop(0, NA, edge_stats, 0)
    lax.fori_loop(0, NA, middle, 0)
    lax.fori_loop(0, NA, foreign, 0)
    lax.fori_loop(0, NA, finish, 0)

    rsend[0] = rk_s[REG_DEV:, :]
    rsend[1] = rv_s[REG_DEV:, :]
    reg_copy = pltpu.make_async_remote_copy(
        rsend, rrecv, lat_ss.at[1], lat_rs.at[1], device_id={"lat": peer}, device_id_type=MESH
    )
    reg_copy.start()
    reg_copy.wait_recv()
    own_k = (rk_s[:REG_DEV, :] + rrecv[0]) / divisor
    own_v = (rv_s[:REG_DEV, :] + rrecv[1]) / divisor
    for a in range(NA):
        for b in range(NB):
            mine = row8 == reg_ref[a, b]
            rep = mrep[a, b * CELLS : (b + 1) * CELLS, :]
            rep2 = jnp.concatenate([rep, rep], axis=1)
            row_k = jnp.sum(jnp.where(mine, own_k, 0.0), axis=0, keepdims=True)
            row_v = jnp.sum(jnp.where(mine, own_v, 0.0), axis=0, keepdims=True)
            dk = dk_s[a, b * CELLS : (b + 1) * CELLS, :] + rep2 * row_k
            dv = dv_s[a, b * CELLS : (b + 1) * CELLS, :] + rep2 * row_v
            o_k[a, :, b] = dk.reshape(WIN, WIN, 256).astype(BF16)
            o_v[a, :, b] = dv.reshape(WIN, WIN, 256).astype(BF16)
    for a in range(NA):
        for side in range(2):
            rows_copy(dq_out, dq_in, dq_ss, dq_rs, 1 - side, a).wait_recv()
        for i, (block, _, _) in enumerate(EDGE):
            side, slot = i // 2, i % 2
            dq = dq_s[a, i] + dq_in[side, a, slot].astype(F32)
            o_q[a, :, block] = dq.reshape(WIN, WIN, 256).astype(BF16)
    for side in range(2):
        for a in range(NA):
            for slot in range(2):
                for kind in range(2):
                    qg_copy(side, a, slot, kind).wait_send()
            rows_copy(st_out, st_in, st_ss, st_rs, side, a).wait_send()
            rows_copy(pst_out, pst_in, pst_ss, pst_rs, side, a).wait_send()
            rows_copy(dq_out, dq_in, dq_ss, dq_rs, side, a).wait_send()
    pool_copy.wait_send()
    reg_copy.wait_send()


def store(a_in, b_in, c_in, a_out, b_out, c_out, sem):
    copies = [
        pltpu.make_async_copy(src, dst, sem.at[i])
        for i, (src, dst) in enumerate(((a_in, a_out), (b_in, b_out), (c_in, c_out)))
    ]
    for copy in copies:
        copy.start()
    for copy in copies:
        copy.wait()


def local(queries, keys, values, grad_out, key_mask, offsets, regions):
    shape = queries.shape
    grid = (NA, WIN, NB, WIN, 256)
    hbm_spec = pl.BlockSpec(memory_space=pltpu.HBM)
    vmem_spec = pl.BlockSpec(memory_space=pltpu.VMEM)
    vm = pltpu.VMEM
    dma = pltpu.SemaphoreType.DMA
    outs = pl.pallas_call(
        kernel,
        out_shape=[jax.ShapeDtypeStruct(grid, BF16)] * 3,
        in_specs=[hbm_spec] * 7,
        out_specs=[vmem_spec] * 3,
        scratch_shapes=[vm(grid, BF16)] * 4
        + [vm((NA, NB * CELLS, 256), BF16)] * 2
        + [vm((NA, NB * CELLS, 128), F32)]
        + [vm((2, NA, 2, WIN, WIN, 256), BF16)] * 2
        + [vm((NA, 4, 4 * CELLS + 2 * REG_DEV, 256), F32)] * 2
        + [vm((NA, NB * CELLS, 256), F32)] * 2
        + [vm((NA, 4, CELLS, 256), F32)]
        + [vm((2 * REG_DEV, 256), F32)] * 2
        + [vm((2, 2, REG_DEV, 256), BF16)]
        + [vm((2, REG_DEV, 256), F32)] * 2
        + [vm((2, NA, 2, 8, 256), F32)] * 4
        + [vm((2, NA, 2, CELLS, 256), BF16)] * 2
        + [vm(key_mask.shape, jnp.int32)]
        + [pltpu.SMEM(offsets.shape, jnp.int32)] * 2
        + [dma((7,))]
        + [dma((2, NA, 2, 2))] * 2
        + [dma((2, NA))] * 6
        + [dma((2,))] * 2,
        compiler_params=pltpu.CompilerParams(
            collective_id=0, has_side_effects=True, vmem_limit_bytes=67108864
        ),
        cost_estimate=pl.CostEstimate(flops=2200000000, bytes_accessed=2300000, transcendentals=860000),
    )(
        *(x.reshape(grid) for x in (queries, keys, values, grad_out)), key_mask, offsets, regions
    )
    return tuple(x.reshape(shape) for x in outs)


def solution(mesh):
    tile = P("lat", "lon", "head")
    cells = P("lat", "lon")
    return jax.shard_map(
        local, mesh=mesh, in_specs=(tile,) * 4 + (cells,) * 3, out_specs=(tile,) * 3, check_vma=False
    )
```

time: 156 us -> 33.9 us (0.22)
  local copies, waits for them, and re-layouts: 72 us -> 3.58 us
  Pallas kernels: 0 us -> 29.5 us
  starting transfers between devices: 24.5 us -> 0 us
  matrix products: 20 us -> 0 us
  other arithmetic: 17.2 us -> 0 us
  between operations: 14.7 us -> 0.65 us
  blocking collectives: 3.59 us -> 0 us
  waiting for transfers between devices: 3.11 us -> 0 us
    pallas_call x0 -> x1, Pallas kernels: none -> 29.5 us  [local(): pl.pallas_call(kernel, out_shape=[jax.ShapeDtypeStruct(grid, BF16)] * 3,...]
    slice x19 -> x0, local copies, waits for them, and re-layouts: 25.1 us -> none  [the longest x10 11.8 us: window_blocks(): extended[:, step:step + lon_blocks]]
    ppermute x10 -> x0, starting transfers between devices: 24.5 us -> none  [the longest x5 22.3 us: extended_2(): lax.ppermute(head, axis, [((i + 1) % count, i) for i in range(count)])]
    dot_general x15 -> x0, matrix products: 20 us -> none  [the longest x1 4.53 us: local(): jnp.einsum('abhqk,abkhd->abqhd', window_lower_bound, candidate_values, pr...]
    unnamed x78 -> x7, local copies, waits for them, and re-layouts: 22.7 us -> 3.58 us
    concatenate x8 -> x0, local copies, waits for them, and re-layouts: 12.5 us -> none  [the longest x7 12.5 us: window_blocks(): jnp.concatenate([extended[:, step:step + lon_blocks] for step in range(5)...]
    add x4 -> x0, other arithmetic: 5.6 us -> none  [the longest x2 5.51 us: fold_blocks(): folded = piece if folded is None else folded + piece]
    scatter-add x4 -> x0, other arithmetic: 3.99 us -> none  [the longest x1 1.89 us: local(): ext_v[:, rim_blocks:-rim_blocks].at[:, :rim_blocks]]
  transfers between devices with their start and end apart: 11 -> 0, of which waited for: 1 -> 0; matrix products, arithmetic and copies ran while one was open for 34% -> 0% of each run, Pallas kernels for 0% -> 0%
where the time goes in v1:
time: 33.9 us; the launch traced here: 33.7 us
  Pallas kernels  29.5 us (87%)
  local copies, waits for them, and re-layouts  3.58 us (11%)
  between operations  0.65 us (2%)
    pallas_call x1, Pallas kernels, local(): pl.pallas_call(kernel, out_shape=[jax.ShapeDtypeStruct(grid, BF16)] * 3,...  29.5 us
    unnamed x7, local copies, waits for them, and re-layouts  3.58 us

profile of v1, /device:TPU:1, one launch (start us, length us, event | category | flops | bytes accessed | tf_op | source)
XLA Modules:
  0.0 33.7 jit_solution(14702481390226330674)
XLA Ops:
  0.6 29.5 %shard_map.94 = (bf16[2,8,5,8,256]{4,3,2,1,0:T(8,128)(2,1)}, bf16[2,8,5,8,256]{4,3,2,1,0:T(8,128)(2,1)}, bf16[2,8,5,8,256]{4,3,2,1,0:T(8,128)(2,1)}) custom-call(bf16[2,8,5,8,256]{4,3,2,1,0:T(8,128)(2,1)} %bitcast.10, bf16[2,8,5,8,256]{4,3,2,1,0:T(8,128)(2,1)} %bitcast.11, bf16[2,8,5,8,256]{4,3,2,1,0:T(8,128)(2,1)} %bitcast.12, ...), custom_call_target="tpu_custom_call" | custom-call | flops 2200000000 | bytes 2300000 | tf_op jit(solution)/shard_map/pallas_call | solution.py:321
  30.1 0.0 copy-start.1
  30.1 1.8 %copy.13 = bf16[16,40,256]{2,1,0:T(8,128)(2,1)} copy(bf16[16,40,256]{2,1,0:T(8,128)(2,1)} %bitcast.9) | data formatting | bytes 655360
  31.9 0.0 copy-done.1
  31.9 0.0 copy-start
  31.9 0.7 %copy.14 = bf16[16,40,256]{2,1,0:T(8,128)(2,1)} copy(bf16[16,40,256]{2,1,0:T(8,128)(2,1)S(1)} %bitcast.8) | data formatting | bytes 655360
  32.6 0.4 %copy-done = bf16[2,8,5,8,256]{4,3,2,1,0:T(8,128)(2,1)S(1)} copy-done((bf16[2,8,5,8,256]{4,3,2,1,0:T(8,128)(2,1)S(1)}, bf16[2,8,5,8,256]{4,3,2,1,0:T(8,128)(2,1)}, u32[]{:S(2)}) %copy-start) | copy-done | bytes 327704
  33.0 0.7 %copy.15 = bf16[16,40,256]{2,1,0:T(8,128)(2,1)} copy(bf16[16,40,256]{2,1,0:T(8,128)(2,1)S(1)} %bitcast.7) | data formatting | bytes 655360
Async XLA Ops:
  30.1 1.8 %copy-start.1 = (bf16[2,8,5,8,256]{4,3,2,1,0:T(8,128)(2,1)S(1)}, bf16[2,8,5,8,256]{4,3,2,1,0:T(8,128)(2,1)}, u32[]{:S(2)}) copy-start(bf16[2,8,5,8,256]{4,3,2,1,0:T(8,128)(2,1)} %get-tuple-element.7) | copy-start | bytes 983044
  31.9 1.1 %copy-start = (bf16[2,8,5,8,256]{4,3,2,1,0:T(8,128)(2,1)S(1)}, bf16[2,8,5,8,256]{4,3,2,1,0:T(8,128)(2,1)}, u32[]{:S(2)}) copy-start(bf16[2,8,5,8,256]{4,3,2,1,0:T(8,128)(2,1)} %get-tuple-element.8) | copy-start | bytes 983044

commit v2 on v1

v2 whole, which is shorter than its diff:
```python
import jax
import jax.numpy as jnp
from jax import lax
from jax.experimental import pallas as pl
from jax.experimental.pallas import tpu as pltpu
from jax.sharding import PartitionSpec as P

HS = 64
WIN = 8
CELLS = WIN * WIN
REG_DEV = 8
NA = 2
NB = 5
VMEM_BYTES = 64 * 1024 * 1024
MASKED = -1.0e30
FLOOR = -1.0e29
SCALE = HS ** (-0.5)
MESH = pl.DeviceIdType.MESH
NT = (((1,), (1,)), ((), ()))
TN = (((0,), (0,)), ((), ()))
F32 = jnp.float32
BF16 = jnp.bfloat16

EDGE = (
    (0, 0, 3, 0, 0, 2, -2), (1, 0, 4, 0, 1, 2, -1),
    (3, 1, 5, 1, 0, 1, 5), (4, 2, 5, 1, 0, 2, 5),
)
FOREIGN = (((0, -2, 0, 1), (1, -1, 0, 2)), ((0, 5, 3, 5), (1, 6, 4, 5)))


def dot(a, b, dims=(((1,), (0,)), ((), ()))):
    return lax.dot_general(a, b, dims, preferred_element_type=F32)


def kernel(
    q_hbm, k_hbm, v_hbm, g_hbm, mask_hbm, off_hbm, reg_hbm,
    oq_hbm, ok_hbm, ov_hbm,
    q_in, k_in, v_in, g_in, kb, vb, mrep, frep,
    fk, fv, fq, fg, fmask, e_s, p_s, dk_s, dv_s, rk_s, rv_s,
    pool, rsend, rrecv, st_out, st_in, o_q, o_k, o_v,
    mask_ref, off_ref, reg_ref,
    in_sem, out_sem, kv_ss, kv_rs, qg_ss, qg_rs, mk_ss, mk_rs, st_ss, st_rs, lat_ss, lat_rs, late,
):
    count = lax.axis_size("lon")
    me = lax.axis_index("lon")
    right = lax.rem(me + 1, count)
    left = lax.rem(me + count - 1, count)
    peer = 1 - lax.axis_index("lat")
    sides = ({"lon": left}, {"lon": right})
    first_tile = me == 0
    last_tile = me == count - 1

    barrier = pltpu.get_barrier_semaphore()
    for device in (sides[0], {"lat": peer}):
        pl.semaphore_signal(barrier, inc=1, device_id=device, device_id_type=MESH)

    @pl.when(jnp.logical_not(last_tile))
    def _():
        pl.semaphore_signal(barrier, inc=1, device_id=sides[1], device_id_type=MESH)

    loads = [
        pltpu.make_async_copy(src, dst, in_sem.at[i])
        for i, (src, dst) in enumerate((
            (mask_hbm, mask_ref), (off_hbm, off_ref), (reg_hbm, reg_ref),
            (k_hbm, k_in), (v_hbm, v_in), (q_hbm, q_in), (g_hbm, g_in),
        ))
    ]
    for copy in loads:
        copy.start()
    pl.semaphore_wait(barrier, jnp.where(first_tile, 2, 3))

    @pl.when(last_tile)
    def _():
        pl.semaphore_signal(late, inc=1, device_id=sides[1], device_id_type=MESH)

    def edge_blocks(side):
        return pl.ds(0 if side == 0 else 3, 2)

    def remote(src, dst, ss, rs, side):
        return pltpu.make_async_remote_copy(
            src, dst, ss, rs, device_id=sides[side], device_id_type=MESH
        )

    def mask_copy(side):
        return remote(mask_hbm, fmask.at[1 - side], mk_ss.at[side], mk_rs.at[1 - side], side)

    def kv_copy(side, kind):
        src = (k_hbm, v_hbm)[kind].at[:, :, edge_blocks(side)]
        dst = (fk, fv)[kind].at[1 - side]
        return remote(src, dst, kv_ss.at[side, kind], kv_rs.at[1 - side, kind], side)

    def qg_copy(side, a, kind):
        src = (q_hbm, g_hbm)[kind].at[a, :, edge_blocks(side)]
        dst = (fq, fg)[kind].at[1 - side, a]
        return remote(src, dst, qg_ss.at[side, a, kind], qg_rs.at[1 - side, a, kind], side)

    def st_copy(side):
        return remote(st_out.at[side], st_in.at[1 - side], st_ss.at[side], st_rs.at[1 - side], side)

    def bulk(side):
        copies = [mask_copy(side)] + [kv_copy(side, kind) for kind in range(2)]
        return copies + [qg_copy(side, a, kind) for a in range(NA) for kind in range(2)]

    for copy in bulk(1):
        copy.start()

    @pl.when(jnp.logical_not(first_tile))
    def _():
        for copy in bulk(0):
            copy.start()

    lane_head = lax.broadcasted_iota(jnp.int32, (CELLS, 4 * HS), 1) // HS
    head_mask = [(lane_head == h).astype(F32).astype(BF16) for h in range(4)]
    low_half = lax.broadcasted_iota(jnp.int32, (CELLS, 128), 1) < HS

    def block_diag(x):
        return jnp.concatenate([x * head_mask[h] for h in range(4)], axis=0)

    def diag_rows(full):
        return jnp.concatenate(
            [
                jnp.where(low_half, full[0:64, 0:128], full[64:128, 0:128]),
                jnp.where(low_half, full[128:192, 128:256], full[192:256, 128:256]),
            ],
            axis=1,
        )

    for copy in loads:
        copy.wait()

    cell_t = lax.broadcasted_iota(jnp.int32, (CELLS, NB * WIN), 0) % WIN
    lane = lax.broadcasted_iota(jnp.int32, (CELLS, NB * WIN), 1)
    row8 = lax.broadcasted_iota(jnp.int32, (REG_DEV, 256), 0)

    def mask_rows(mask8):
        mask8 = mask8.astype(F32)
        return jnp.broadcast_to(mask8[:, None, :], (WIN, WIN, NB * WIN)).reshape(CELLS, NB * WIN)

    def mask_cells(mask64, b):
        column = jnp.sum(jnp.where(lane == cell_t + b * WIN, mask64, 0.0), axis=1, keepdims=True)
        return jnp.broadcast_to(column, (CELLS, 128))

    pk = jnp.zeros((REG_DEV, 256), F32)
    pv = jnp.zeros((REG_DEV, 256), F32)
    cnt = jnp.zeros((REG_DEV, 256), F32)
    for a in range(NA):
        mask64 = mask_rows(mask_ref[a * WIN : (a + 1) * WIN, :])
        for b in range(NB):
            rep = mask_cells(mask64, b)
            mrep[a, b * CELLS : (b + 1) * CELLS, :] = rep
            rep2 = jnp.concatenate([rep, rep], axis=1)
            kx = k_in[a, :, b].reshape(CELLS, 256)
            vx = v_in[a, :, b].reshape(CELLS, 256)
            kb[a, b * CELLS : (b + 1) * CELLS, :] = kx
            vb[a, b * CELLS : (b + 1) * CELLS, :] = vx
            mine = row8 == reg_ref[a, b]
            pk = pk + jnp.where(mine, jnp.sum(kx.astype(F32) * rep2, axis=0, keepdims=True), 0.0)
            pv = pv + jnp.where(mine, jnp.sum(vx.astype(F32) * rep2, axis=0, keepdims=True), 0.0)
            cnt = cnt + jnp.where(mine, jnp.sum(rep2, axis=0, keepdims=True), 0.0)
    divisor = jnp.maximum(cnt, 1.0)
    pool[0, 0] = (pk / divisor).astype(BF16)
    pool[0, 1] = (pv / divisor).astype(BF16)
    pool_copy = pltpu.make_async_remote_copy(
        pool.at[0], pool.at[1], lat_ss.at[0], lat_rs.at[0], device_id={"lat": peer}, device_id_type=MESH
    )
    pool_copy.start()
    dk_s[...] = jnp.zeros_like(dk_s)
    dv_s[...] = jnp.zeros_like(dv_s)
    rk_s[...] = jnp.zeros_like(rk_s)
    rv_s[...] = jnp.zeros_like(rv_s)
    pool_copy.wait_recv()
    reg_k = jnp.concatenate([pool[0, 0].astype(F32), pool[1, 0].astype(F32)], axis=0).astype(BF16)
    reg_v = jnp.concatenate([pool[0, 1].astype(F32), pool[1, 1].astype(F32)], axis=0).astype(BF16)

    def bias(rep, relative, start):
        row = lax.broadcasted_iota(jnp.int32, rep.shape, 0)
        key_off = row // CELLS * WIN + row % WIN + relative * WIN
        usable = (key_off >= start - WIN) & (key_off < start + 2 * WIN) & (rep > 0.5)
        half = jnp.where(usable, 0.0, MASKED)
        return jnp.concatenate([half, half], axis=1)

    def partial_stats(keys, values, bdq, bdg, add):
        s = dot(keys, bdq, NT) + add
        dp = dot(values, bdg, NT)
        top = jnp.maximum(jnp.max(s, axis=0, keepdims=True), FLOOR)
        e = jnp.exp(s - top)
        total = jnp.sum(e, axis=0, keepdims=True)
        inner = jnp.sum(e * dp, axis=0, keepdims=True)
        return e, dp, (top, total, inner)

    def merged(x, y):
        top = jnp.maximum(x[0], y[0])
        fx = jnp.exp(x[0] - top)
        fy = jnp.exp(y[0] - top)
        inverse = 1.0 / (x[1] * fx + y[1] * fy)
        return fx * inverse, fy * inverse, (x[2] * fx + y[2] * fy) * inverse

    def weights(e, dp, alpha, delta):
        p = e * alpha
        ds = p * (dp - delta)
        return p.astype(BF16), ds.astype(BF16)

    def add_key_grads(a, first, end, p, ds, bdq, bdg, regs):
        rows = (end - first) * CELLS
        dv = dot(p, bdg)
        dk = dot(ds, bdq)
        dv_s[a, first * CELLS : end * CELLS, :] += dv[:rows]
        dk_s[a, first * CELLS : end * CELLS, :] += dk[:rows]
        if regs:
            rv_s[...] += dv[rows:]
            rk_s[...] += dk[rows:]

    def diag_pair(q, g):
        bdq = block_diag(q.reshape(CELLS, 256) * jnp.asarray(SCALE, BF16))
        return bdq, block_diag(g.reshape(CELLS, 256))

    def local_q(a, block):
        return diag_pair(q_in[a, :, block], g_in[a, :, block])

    def local_keys(a, first, end):
        keys = jnp.concatenate([kb[a, first * CELLS : end * CELLS, :], reg_k], axis=0)
        values = jnp.concatenate([vb[a, first * CELLS : end * CELLS, :], reg_v], axis=0)
        return keys, values

    def local_stats(a, block, first, end):
        keys, values = local_keys(a, first, end)
        bdq, bdg = local_q(a, block)
        rep = mrep[a, first * CELLS : end * CELLS, :]
        add = jnp.concatenate(
            [bias(rep, first - block, off_ref[a, block]), jnp.zeros((2 * REG_DEV, 256), F32)], axis=0
        )
        e, dp, stats = partial_stats(keys, values, bdq, bdg, add)
        return keys, bdq, bdg, e, dp, stats

    def edge_stats(a, carry):
        for i, (block, first, end, side, _, _, _) in enumerate(EDGE):
            rows = (end - first) * CELLS + 2 * REG_DEV
            _, _, _, e, dp, stats = local_stats(a, block, first, end)
            e_s[a, i, :rows] = e
            p_s[a, i, :rows] = dp
            slot = i % 2
            for r in range(3):
                st_out[side, a, slot, r : r + 1] = stats[r]
            st_out[side, a, slot, 3:4] = jnp.full((1, 256), off_ref[a, block], jnp.int32).astype(F32)
        return carry

    def middle(a, carry):
        keys, bdq, bdg, e, dp, stats = local_stats(a, 2, 0, NB)
        inverse = 1.0 / stats[1]
        p, ds = weights(e, dp, inverse, stats[2] * inverse)
        add_key_grads(a, 0, NB, p, ds, bdq, bdg, True)
        dq = diag_rows(dot(ds, keys, TN)) * SCALE
        o_q[a, :, 2] = dq.reshape(WIN, WIN, 256).astype(BF16)
        return carry

    def foreign_keys(side):
        mask_copy(1 - side).wait_recv()
        for kind in range(2):
            kv_copy(1 - side, kind).wait_recv()

        def body(a, carry):
            mask64 = mask_rows(fmask[side, pl.ds(pl.multiple_of(a * WIN, WIN), WIN), :])
            for slot in range(2):
                frep[slot * CELLS : (slot + 1) * CELLS, :] = mask_cells(mask64, slot + (3 if side == 0 else 0))
            for i, (block, first, end, edge_side, low, high, relative) in enumerate(EDGE):
                if edge_side != side:
                    continue
                rows = (end - first) * CELLS + 2 * REG_DEV
                far_k = jnp.concatenate(
                    [fk[side, a, :, slot].reshape(CELLS, 256) for slot in range(low, high)], axis=0
                )
                far_v = jnp.concatenate(
                    [fv[side, a, :, slot].reshape(CELLS, 256) for slot in range(low, high)], axis=0
                )
                keys, _ = local_keys(a, first, end)
                bdq, bdg = local_q(a, block)
                add = bias(frep[low * CELLS : high * CELLS, :], relative - block, off_ref[a, block])
                far_e, far_dp, far = partial_stats(far_k, far_v, bdq, bdg, add)
                near = tuple(st_out[side, a, i % 2, r : r + 1] for r in range(3))
                alpha, far_alpha, delta = merged(near, far)
                p, ds = weights(e_s[a, i, :rows], p_s[a, i, :rows], alpha, delta)
                _, far_ds = weights(far_e, far_dp, far_alpha, delta)
                dq = diag_rows(dot(ds, keys, TN) + dot(far_ds, far_k, TN)) * SCALE
                add_key_grads(a, first, end, p, ds, bdq, bdg, True)
                o_q[a, :, block] = dq.reshape(WIN, WIN, 256).astype(BF16)
            return carry

        lax.fori_loop(0, NA, body, 0)

    def foreign_queries(side):
        st_copy(1 - side).wait_recv()

        def body(a, carry):
            for kind in range(2):
                qg_copy(1 - side, a, kind).wait_recv()
            for slot, block, first, end in FOREIGN[side]:
                keys = kb[a, first * CELLS : end * CELLS, :]
                values = vb[a, first * CELLS : end * CELLS, :]
                bdq, bdg = diag_pair(fq[side, a, :, slot], fg[side, a, :, slot])
                theirs = tuple(st_in[side, a, slot, r : r + 1] for r in range(3))
                start = st_in[side, a, slot, 3:4, 0:128].astype(jnp.int32)
                add = bias(mrep[a, first * CELLS : end * CELLS, :], first - block, start)
                e, dp, stats = partial_stats(keys, values, bdq, bdg, add)
                alpha, _, delta = merged(stats, theirs)
                p, ds = weights(e, dp, alpha, delta)
                add_key_grads(a, first, end, p, ds, bdq, bdg, False)
            return carry

        lax.fori_loop(0, NA, body, 0)

    lax.fori_loop(0, NA, edge_stats, 0)
    st_copy(1).start()

    @pl.when(jnp.logical_not(first_tile))
    def _():
        st_copy(0).start()

    lax.fori_loop(0, NA, middle, 0)

    @pl.when(first_tile)
    def _():
        pl.semaphore_wait(late, 1)
        for copy in bulk(0) + [st_copy(0)]:
            copy.start()

    foreign_keys(1)
    foreign_keys(0)

    out_q = pltpu.make_async_copy(o_q, oq_hbm, out_sem.at[0])
    out_q.start()
    rsend[0] = rk_s[REG_DEV:, :]
    rsend[1] = rv_s[REG_DEV:, :]
    reg_copy = pltpu.make_async_remote_copy(
        rsend, rrecv, lat_ss.at[1], lat_rs.at[1], device_id={"lat": peer}, device_id_type=MESH
    )
    reg_copy.start()
    foreign_queries(1)
    reg_copy.wait_recv()
    own_k = (rk_s[:REG_DEV, :] + rrecv[0]) / divisor
    own_v = (rv_s[:REG_DEV, :] + rrecv[1]) / divisor
    for a in range(NA):
        for b in range(NB):
            mine = row8 == reg_ref[a, b]
            rep = mrep[a, b * CELLS : (b + 1) * CELLS, :]
            rep2 = jnp.concatenate([rep, rep], axis=1)
            for own, total, out in ((own_k, dk_s, o_k), (own_v, dv_s, o_v)):
                row = jnp.sum(jnp.where(mine, own, 0.0), axis=0, keepdims=True)
                cells = total[a, b * CELLS : (b + 1) * CELLS, :] + rep2 * row
                if b < 2:
                    total[a, b * CELLS : (b + 1) * CELLS, :] = cells
                else:
                    out[a, :, b] = cells.reshape(WIN, WIN, 256).astype(BF16)

    foreign_queries(0)
    for a in range(NA):
        for b in range(2):
            for total, out in ((dk_s, o_k), (dv_s, o_v)):
                cells = total[a, b * CELLS : (b + 1) * CELLS, :]
                out[a, :, b] = cells.reshape(WIN, WIN, 256).astype(BF16)
    out_k = pltpu.make_async_copy(o_k, ok_hbm, out_sem.at[1])
    out_v = pltpu.make_async_copy(o_v, ov_hbm, out_sem.at[2])
    out_k.start()
    out_v.start()
    for side in range(2):
        for copy in bulk(side) + [st_copy(side)]:
            copy.wait_send()
    pool_copy.wait_send()
    reg_copy.wait_send()
    out_q.wait()
    out_k.wait()
    out_v.wait()


def store(a_in, b_in, c_in, a_out, b_out, c_out, stage, in_sem, out_sem):
    ins = (a_in, b_in, c_in)
    outs = (a_out, b_out, c_out)
    reads = [pltpu.make_async_copy(ins[i], stage.at[i], in_sem.at[i]) for i in range(3)]
    writes = [pltpu.make_async_copy(stage.at[i], outs[i], out_sem.at[i]) for i in range(3)]
    for copy in reads:
        copy.start()
    for read, write in zip(reads, writes):
        read.wait()
        write.start()
    for copy in writes:
        copy.wait()


def local(queries, keys, values, grad_out, key_mask, offsets, regions):
    shape = queries.shape
    grid = (NA, WIN, NB, WIN, 256)
    edge = (2, NA, WIN, 2, WIN, 256)
    hbm_spec = pl.BlockSpec(memory_space=pltpu.HBM)
    vm = pltpu.VMEM
    dma = pltpu.SemaphoreType.DMA
    outs = pl.pallas_call(
        kernel,
        out_shape=[jax.ShapeDtypeStruct(grid, BF16)] * 3,
        in_specs=[hbm_spec] * 7,
        out_specs=[hbm_spec] * 3,
        scratch_shapes=[vm(grid, BF16)] * 4
        + [vm((NA, NB * CELLS, 256), BF16)] * 2
        + [vm((NA, NB * CELLS, 128), F32), vm((2 * CELLS, 128), F32)]
        + [vm(edge, BF16)] * 4
        + [vm((2,) + key_mask.shape, jnp.int32)]
        + [vm((NA, 4, 4 * CELLS + 2 * REG_DEV, 256), F32)] * 2
        + [vm((NA, NB * CELLS, 256), F32)] * 2
        + [vm((2 * REG_DEV, 256), F32)] * 2
        + [vm((2, 2, REG_DEV, 256), BF16)]
        + [vm((2, REG_DEV, 256), F32)] * 2
        + [vm((2, NA, 2, 8, 256), F32)] * 2
        + [vm(grid, BF16)] * 3
        + [vm(key_mask.shape, jnp.int32)]
        + [pltpu.SMEM(offsets.shape, jnp.int32)] * 2
        + [dma((7,)), dma((3,))]
        + [dma((2, 2))] * 2
        + [dma((2, NA, 2))] * 2
        + [dma((2,))] * 6
        + [pltpu.SemaphoreType.REGULAR],
        compiler_params=pltpu.CompilerParams(
            collective_id=0, has_side_effects=True, vmem_limit_bytes=VMEM_BYTES
        ),
        cost_estimate=pl.CostEstimate(flops=2200000000, bytes_accessed=2300000, transcendentals=860000),
    )(
        *(x.reshape(grid) for x in (queries, keys, values, grad_out)), key_mask, offsets, regions
    )
    outs = pl.pallas_call(
        store,
        out_shape=[jax.ShapeDtypeStruct(grid, BF16)] * 3,
        in_specs=[hbm_spec] * 3,
        out_specs=[hbm_spec] * 3,
        scratch_shapes=[vm((3,) + grid, BF16), dma((3,)), dma((3,))],
        compiler_params=pltpu.CompilerParams(vmem_limit_bytes=VMEM_BYTES),
    )(*outs)
    return tuple(x.reshape(shape) for x in outs)


def solution(mesh):
    tile = P("lat", "lon", "head")
    cells = P("lat", "lon")
    return jax.shard_map(
        local, mesh=mesh, in_specs=(tile,) * 4 + (cells,) * 3, out_specs=(tile,) * 3, check_vma=False
    )
```

time: 33.9 us -> 27.4 us (0.81)
  local copies, waits for them, and re-layouts: 3.58 us -> 0 us
  Pallas kernels: 29.5 us -> 26.7 us
    pallas_call x1, Pallas kernels: 29.5 us -> 24.7 us  [local(): pl.pallas_call(kernel, out_shape=[jax.ShapeDtypeStruct(grid, BF16)] * 3,...]
    unnamed x7 -> x0, local copies, waits for them, and re-layouts: 3.58 us -> none
    pallas_call x0 -> x1, Pallas kernels: none -> 1.96 us  [local(): pl.pallas_call(store, out_shape=[jax.ShapeDtypeStruct(grid, BF16)] * 3, i...]
where the time goes in v2:
time: 27.4 us; the launch traced here: 27.3 us
  Pallas kernels  26.7 us (97%)
  between operations  0.64 us (2%)
    pallas_call x1, Pallas kernels, local(): pl.pallas_call(kernel, out_shape=[jax.ShapeDtypeStruct(grid, BF16)] * 3,...  24.7 us
    pallas_call x1, Pallas kernels, local(): pl.pallas_call(store, out_shape=[jax.ShapeDtypeStruct(grid, BF16)] * 3, i...  1.96 us

profile of v2, /device:TPU:1, one launch (start us, length us, event | category | flops | bytes accessed | tf_op | source)
XLA Modules:
  0.0 27.3 jit_solution(6084927292972830987)
XLA Ops:
  0.6 24.7 %shard_map.94 = (bf16[2,8,5,8,256]{4,3,2,1,0:T(8,128)(2,1)}, bf16[2,8,5,8,256]{4,3,2,1,0:T(8,128)(2,1)}, bf16[2,8,5,8,256]{4,3,2,1,0:T(8,128)(2,1)}) custom-call(bf16[2,8,5,8,256]{4,3,2,1,0:T(8,128)(2,1)} %bitcast.7, bf16[2,8,5,8,256]{4,3,2,1,0:T(8,128)(2,1)} %bitcast.8, bf16[2,8,5,8,256]{4,3,2,1,0:T(8,128)(2,1)} %bitcast.9, ...), custom_call_target="tpu_custom_call" | custom-call | flops 2200000000 | bytes 2300000 | tf_op jit(solution)/shard_map/pallas_call | solution.py:395
  25.3 2.0 %shard_map.95 = (bf16[2,8,5,8,256]{4,3,2,1,0:T(8,128)(2,1)}, bf16[2,8,5,8,256]{4,3,2,1,0:T(8,128)(2,1)}, bf16[2,8,5,8,256]{4,3,2,1,0:T(8,128)(2,1)}) custom-call(bf16[2,8,5,8,256]{4,3,2,1,0:T(8,128)(2,1)} %get-tuple-element.9.a_in, bf16[2,8,5,8,256]{4,3,2,1,0:T(8,128)(2,1)} %get-tuple-element.10.b_in, bf16[2,8,5,8,256]{4,3,2,1,0:T(8,128)(2,1)} %get-tuple-element.11.c_in), custom_call_target="tpu_custom_call" | custom-call | tf_op jit(solution)/shard_map/pallas_call | solution.py:426

commit v3 on v2

--- a/solution.py
+++ b/solution.py
@@ -11,7 +11,7 @@
 REG_DEV = 8
 NA = 2
 NB = 5
-VMEM_BYTES = 64 * 1024 * 1024
+VMEM_BYTES = 64236 * 1024
 MASKED = -1.0e30
 FLOOR = -1.0e29
 SCALE = HS ** (-0.5)
@@ -34,12 +34,12 @@
 
 def kernel(
     q_hbm, k_hbm, v_hbm, g_hbm, mask_hbm, off_hbm, reg_hbm,
-    oq_hbm, ok_hbm, ov_hbm,
+    o_q, o_k, o_v,
     q_in, k_in, v_in, g_in, kb, vb, mrep, frep,
     fk, fv, fq, fg, fmask, e_s, p_s, dk_s, dv_s, rk_s, rv_s,
-    pool, rsend, rrecv, st_out, st_in, o_q, o_k, o_v,
+    pool, rsend, rrecv, st_out, st_in,
     mask_ref, off_ref, reg_ref,
-    in_sem, out_sem, kv_ss, kv_rs, qg_ss, qg_rs, mk_ss, mk_rs, st_ss, st_rs, lat_ss, lat_rs, late,
+    in_sem, kv_ss, kv_rs, qg_ss, qg_rs, mk_ss, mk_rs, st_ss, st_rs, lat_ss, lat_rs, late,
 ):
     count = lax.axis_size("lon")
     me = lax.axis_index("lon")
@@ -326,8 +326,6 @@
     foreign_keys(1)
     foreign_keys(0)
 
-    out_q = pltpu.make_async_copy(o_q, oq_hbm, out_sem.at[0])
-    out_q.start()
     rsend[0] = rk_s[REG_DEV:, :]
     rsend[1] = rv_s[REG_DEV:, :]
     reg_copy = pltpu.make_async_remote_copy(
@@ -357,31 +355,19 @@
             for total, out in ((dk_s, o_k), (dv_s, o_v)):
                 cells = total[a, b * CELLS : (b + 1) * CELLS, :]
                 out[a, :, b] = cells.reshape(WIN, WIN, 256).astype(BF16)
-    out_k = pltpu.make_async_copy(o_k, ok_hbm, out_sem.at[1])
-    out_v = pltpu.make_async_copy(o_v, ov_hbm, out_sem.at[2])
-    out_k.start()
-    out_v.start()
     for side in range(2):
         for copy in bulk(side) + [st_copy(side)]:
             copy.wait_send()
     pool_copy.wait_send()
     reg_copy.wait_send()
-    out_q.wait()
-    out_k.wait()
-    out_v.wait()
-
-
-def store(a_in, b_in, c_in, a_out, b_out, c_out, stage, in_sem, out_sem):
-    ins = (a_in, b_in, c_in)
-    outs = (a_out, b_out, c_out)
-    reads = [pltpu.make_async_copy(ins[i], stage.at[i], in_sem.at[i]) for i in range(3)]
-    writes = [pltpu.make_async_copy(stage.at[i], outs[i], out_sem.at[i]) for i in range(3)]
-    for copy in reads:
+
+
+def store(a_in, b_in, c_in, a_out, b_out, c_out, sem):
+    pairs = ((a_in, a_out), (b_in, b_out), (c_in, c_out))
+    copies = [pltpu.make_async_copy(src, dst, sem.at[i]) for i, (src, dst) in enumerate(pairs)]
+    for copy in copies:
         copy.start()
-    for read, write in zip(reads, writes):
-        read.wait()
-        write.start()
-    for copy in writes:
+    for copy in copies:
         copy.wait()
 
 
@@ -394,9 +380,9 @@
     dma = pltpu.SemaphoreType.DMA
     outs = pl.pallas_call(
         kernel,
-        out_shape=[jax.ShapeDtypeStruct(grid, BF16)] * 3,
+        out_shape=[pltpu.VMEM(grid, BF16)] * 3,
         in_specs=[hbm_spec] * 7,
-        out_specs=[hbm_spec] * 3,
+        out_specs=[pl.BlockSpec(memory_space=pltpu.VMEM)] * 3,
         scratch_shapes=[vm(grid, BF16)] * 4
         + [vm((NA, NB * CELLS, 256), BF16)] * 2
         + [vm((NA, NB * CELLS, 128), F32), vm((2 * CELLS, 128), F32)]
@@ -408,10 +394,9 @@
         + [vm((2, 2, REG_DEV, 256), BF16)]
         + [vm((2, REG_DEV, 256), F32)] * 2
         + [vm((2, NA, 2, 8, 256), F32)] * 2
-        + [vm(grid, BF16)] * 3
         + [vm(key_mask.shape, jnp.int32)]
         + [pltpu.SMEM(offsets.shape, jnp.int32)] * 2
-        + [dma((7,)), dma((3,))]
+        + [dma((7,))]
         + [dma((2, 2))] * 2
         + [dma((2, NA, 2))] * 2
         + [dma((2,))] * 6
@@ -426,10 +411,10 @@
     outs = pl.pallas_call(
         store,
         out_shape=[jax.ShapeDtypeStruct(grid, BF16)] * 3,
-        in_specs=[hbm_spec] * 3,
+        in_specs=[pl.BlockSpec(memory_space=pl.ANY)] * 3,
         out_specs=[hbm_spec] * 3,
-        scratch_shapes=[vm((3,) + grid, BF16), dma((3,)), dma((3,))],
-        compiler_params=pltpu.CompilerParams(vmem_limit_bytes=VMEM_BYTES),
+        scratch_shapes=[dma((3,))],
+        compiler_params=pltpu.CompilerParams(vmem_limit_bytes=1024 * 1024),
     )(*outs)
     return tuple(x.reshape(shape) for x in outs)
 

time: 27.4 us -> 25.6 us (0.934)
  Pallas kernels: 26.7 us -> 24.8 us
    pallas_call x1, Pallas kernels: 1.96 us -> 0.97 us  [local(): pl.pallas_call(store, out_shape=[jax.ShapeDtypeStruct(grid, BF16)] * 3, i...]
    pallas_call x1, Pallas kernels: 24.7 us -> 23.9 us  [local(): pl.pallas_call(kernel, out_shape=[pltpu.VMEM(grid, BF16)] * 3, in_specs=[...]
where the time goes in v3:
time: 25.6 us; the launch traced here: 25.5 us
  Pallas kernels  24.8 us (97%)
  between operations  0.64 us (2%)
    pallas_call x1, Pallas kernels, local(): pl.pallas_call(kernel, out_shape=[pltpu.VMEM(grid, BF16)] * 3, in_specs=[...  23.9 us
    pallas_call x1, Pallas kernels, local(): pl.pallas_call(store, out_shape=[jax.ShapeDtypeStruct(grid, BF16)] * 3, i...  0.97 us

profile of v3, /device:TPU:1, one launch (start us, length us, event | category | flops | bytes accessed | tf_op | source)
XLA Modules:
  0.0 25.5 jit_solution(7241321013134456709)
XLA Ops:
  0.6 23.9 %shard_map.94 = (bf16[2,8,5,8,256]{4,3,2,1,0:T(8,128)(2,1)S(1)}, bf16[2,8,5,8,256]{4,3,2,1,0:T(8,128)(2,1)S(1)}, bf16[2,8,5,8,256]{4,3,2,1,0:T(8,128)(2,1)S(1)}) custom-call(bf16[2,8,5,8,256]{4,3,2,1,0:T(8,128)(2,1)} %bitcast.7, bf16[2,8,5,8,256]{4,3,2,1,0:T(8,128)(2,1)} %bitcast.8, bf16[2,8,5,8,256]{4,3,2,1,0:T(8,128)(2,1)} %bitcast.9, ...), custom_call_target="tpu_custom_call" | custom-call | flops 2200000000 | bytes 2300000 | tf_op jit(solution)/shard_map/pallas_call | solution.py:381
  24.5 1.0 %shard_map.95 = (bf16[2,8,5,8,256]{4,3,2,1,0:T(8,128)(2,1)}, bf16[2,8,5,8,256]{4,3,2,1,0:T(8,128)(2,1)}, bf16[2,8,5,8,256]{4,3,2,1,0:T(8,128)(2,1)}) custom-call(bf16[2,8,5,8,256]{4,3,2,1,0:T(8,128)(2,1)S(1)} %get-tuple-element.9.a_in, bf16[2,8,5,8,256]{4,3,2,1,0:T(8,128)(2,1)S(1)} %get-tuple-element.10.b_in, ...), custom_call_target="tpu_custom_call" | custom-call | tf_op jit(solution)/shard_map/pallas_call | solution.py:411

commit v4 on v3

--- a/solution.py
+++ b/solution.py
@@ -11,7 +11,7 @@
 REG_DEV = 8
 NA = 2
 NB = 5
-VMEM_BYTES = 64236 * 1024
+VMEM_BYTES = 56 * 1024 * 1024
 MASKED = -1.0e30
 FLOOR = -1.0e29
 SCALE = HS ** (-0.5)
@@ -25,7 +25,6 @@
     (0, 0, 3, 0, 0, 2, -2), (1, 0, 4, 0, 1, 2, -1),
     (3, 1, 5, 1, 0, 1, 5), (4, 2, 5, 1, 0, 2, 5),
 )
-FOREIGN = (((0, -2, 0, 1), (1, -1, 0, 2)), ((0, 5, 3, 5), (1, 6, 4, 5)))
 
 
 def dot(a, b, dims=(((1,), (0,)), ((), ()))):
@@ -39,7 +38,7 @@
     fk, fv, fq, fg, fmask, e_s, p_s, dk_s, dv_s, rk_s, rv_s,
     pool, rsend, rrecv, st_out, st_in,
     mask_ref, off_ref, reg_ref,
-    in_sem, kv_ss, kv_rs, qg_ss, qg_rs, mk_ss, mk_rs, st_ss, st_rs, lat_ss, lat_rs, late,
+    in_sem, kv_ss, kv_rs, qg_ss, qg_rs, mk_ss, mk_rs, st_ss, st_rs, lat_ss, lat_rs, late, go, chain, peer_in,
 ):
     count = lax.axis_size("lon")
     me = lax.axis_index("lon")
@@ -50,13 +49,29 @@
     first_tile = me == 0
     last_tile = me == count - 1
 
+    before_last = me == count - 2
+
     barrier = pltpu.get_barrier_semaphore()
-    for device in (sides[0], {"lat": peer}):
-        pl.semaphore_signal(barrier, inc=1, device_id=device, device_id_type=MESH)
+    pl.semaphore_signal(barrier, inc=1, device_id=sides[0], device_id_type=MESH)
+
+    @pl.when(me < count - 2)
+    def _():
+        pl.semaphore_signal(barrier, inc=1, device_id=sides[1], device_id_type=MESH)
 
     @pl.when(jnp.logical_not(last_tile))
     def _():
-        pl.semaphore_signal(barrier, inc=1, device_id=sides[1], device_id_type=MESH)
+        pl.semaphore_signal(barrier, inc=1, device_id={"lat": peer}, device_id_type=MESH)
+
+    pl.semaphore_wait(barrier, jnp.where(last_tile, 1, jnp.where(first_tile, 2, 3)))
+
+    @pl.when(last_tile)
+    def _():
+        pl.semaphore_signal(late, inc=1, device_id=sides[1], device_id_type=MESH)
+
+    @pl.when(before_last)
+    def _():
+        pl.semaphore_signal(chain, inc=1, device_id={"lat": peer}, device_id_type=MESH)
+        pl.semaphore_signal(go, inc=1, device_id=sides[1], device_id_type=MESH)
 
     loads = [
         pltpu.make_async_copy(src, dst, in_sem.at[i])
@@ -65,20 +80,13 @@
             (k_hbm, k_in), (v_hbm, v_in), (q_hbm, q_in), (g_hbm, g_in),
         ))
     ]
-    for copy in loads:
-        copy.start()
-    pl.semaphore_wait(barrier, jnp.where(first_tile, 2, 3))
-
-    @pl.when(last_tile)
-    def _():
-        pl.semaphore_signal(late, inc=1, device_id=sides[1], device_id_type=MESH)
 
     def edge_blocks(side):
-        return pl.ds(0 if side == 0 else 3, 2)
+        return pl.ds(3 * side, 2)
 
     def remote(src, dst, ss, rs, side):
         return pltpu.make_async_remote_copy(
-            src, dst, ss, rs, device_id=sides[side], device_id_type=MESH
+            src, dst, ss, rs, device_id={"lon": jnp.where(side == 0, left, right)}, device_id_type=MESH
         )
 
     def mask_copy(side):
@@ -97,17 +105,25 @@
     def st_copy(side):
         return remote(st_out.at[side], st_in.at[1 - side], st_ss.at[side], st_rs.at[1 - side], side)
 
-    def bulk(side):
-        copies = [mask_copy(side)] + [kv_copy(side, kind) for kind in range(2)]
-        return copies + [qg_copy(side, a, kind) for a in range(NA) for kind in range(2)]
-
-    for copy in bulk(1):
+    def early(side):
+        copies = [kv_copy(side, kind) for kind in range(2)] + [mask_copy(side)]
+        return copies + [qg_copy(side, 0, kind) for kind in range(2)]
+
+    def later(side):
+        return [st_copy(side)] + [qg_copy(side, 1, kind) for kind in range(2)]
+
+    for copy in early(1) + loads:
         copy.start()
 
-    @pl.when(jnp.logical_not(first_tile))
-    def _():
-        for copy in bulk(0):
+    @pl.when(jnp.logical_not(first_tile | last_tile))
+    def _():
+        for copy in early(0):
             copy.start()
+
+    @pl.when(before_last)
+    def _():
+        pl.semaphore_wait(chain, 1)
+        pl.semaphore_signal(peer_in, inc=1, device_id=sides[1], device_id_type=MESH)
 
     lane_head = lax.broadcasted_iota(jnp.int32, (CELLS, 4 * HS), 1) // HS
     head_mask = [(lane_head == h).astype(F32).astype(BF16) for h in range(4)]
@@ -163,6 +179,14 @@
     pool_copy = pltpu.make_async_remote_copy(
         pool.at[0], pool.at[1], lat_ss.at[0], lat_rs.at[0], device_id={"lat": peer}, device_id_type=MESH
     )
+
+    @pl.when(last_tile)
+    def _():
+        pl.semaphore_wait(go, 1)
+        for copy in early(0):
+            copy.start()
+        pl.semaphore_wait(peer_in, 1)
+
     pool_copy.start()
     dk_s[...] = jnp.zeros_like(dk_s)
     dv_s[...] = jnp.zeros_like(dv_s)
@@ -287,76 +311,95 @@
 
         lax.fori_loop(0, NA, body, 0)
 
-    def foreign_queries(side):
-        st_copy(1 - side).wait_recv()
-
-        def body(a, carry):
-            for kind in range(2):
-                qg_copy(1 - side, a, kind).wait_recv()
-            for slot, block, first, end in FOREIGN[side]:
-                keys = kb[a, first * CELLS : end * CELLS, :]
-                values = vb[a, first * CELLS : end * CELLS, :]
-                bdq, bdg = diag_pair(fq[side, a, :, slot], fg[side, a, :, slot])
-                theirs = tuple(st_in[side, a, slot, r : r + 1] for r in range(3))
-                start = st_in[side, a, slot, 3:4, 0:128].astype(jnp.int32)
-                add = bias(mrep[a, first * CELLS : end * CELLS, :], first - block, start)
-                e, dp, stats = partial_stats(keys, values, bdq, bdg, add)
-                alpha, _, delta = merged(stats, theirs)
-                p, ds = weights(e, dp, alpha, delta)
-                add_key_grads(a, first, end, p, ds, bdq, bdg, False)
-            return carry
-
-        lax.fori_loop(0, NA, body, 0)
+    def foreign_queries(side, a):
+        for kind in range(2):
+            qg_copy(1 - side, a, kind).wait_recv()
+        for blocks in range(1, 3):
+            slot = blocks - 1 + side * (3 - 2 * blocks)
+            first = side * (NB - blocks)
+            relative = jnp.where(side == 0, blocks - 3, 7 - blocks)
+            cells = pl.ds(pl.multiple_of(first * CELLS, CELLS), blocks * CELLS)
+            bdq, bdg = diag_pair(fq[side, a, :, slot], fg[side, a, :, slot])
+            theirs = tuple(st_in[side, a, slot, r : r + 1] for r in range(3))
+            start = st_in[side, a, slot, 3:4, 0:128].astype(jnp.int32)
+            add = bias(mrep[a, cells, :], first - relative, start)
+            e, dp, stats = partial_stats(kb[a, cells, :], vb[a, cells, :], bdq, bdg, add)
+            alpha, _, delta = merged(stats, theirs)
+            p, ds = weights(e, dp, alpha, delta)
+            dv_s[a, cells, :] += dot(p, bdg)
+            dk_s[a, cells, :] += dot(ds, bdq)
+
+    def spread(a, low, high):
+        for b in range(low, high):
+            mine = row8 == reg_ref[a, b]
+            rep = mrep[a, b * CELLS : (b + 1) * CELLS, :]
+            rep2 = jnp.concatenate([rep, rep], axis=1)
+            for own, total, out in ((rrecv[0], dk_s, o_k), (rrecv[1], dv_s, o_v)):
+                row = jnp.sum(jnp.where(mine, own, 0.0), axis=0, keepdims=True)
+                cells = total[a, b * CELLS : (b + 1) * CELLS, :] + rep2 * row
+                out[a, :, b] = cells.reshape(WIN, WIN, 256).astype(BF16)
 
     lax.fori_loop(0, NA, edge_stats, 0)
-    st_copy(1).start()
+    for copy in later(1):
+        copy.start()
 
     @pl.when(jnp.logical_not(first_tile))
     def _():
-        st_copy(0).start()
+        for copy in later(0):
+            copy.start()
 
     lax.fori_loop(0, NA, middle, 0)
 
     @pl.when(first_tile)
     def _():
         pl.semaphore_wait(late, 1)
-        for copy in bulk(0) + [st_copy(0)]:
+        for copy in early(0) + later(0):
             copy.start()
 
-    foreign_keys(1)
-    foreign_keys(0)
-
-    rsend[0] = rk_s[REG_DEV:, :]
-    rsend[1] = rv_s[REG_DEV:, :]
     reg_copy = pltpu.make_async_remote_copy(
         rsend, rrecv, lat_ss.at[1], lat_rs.at[1], device_id={"lat": peer}, device_id_type=MESH
     )
-    reg_copy.start()
-    foreign_queries(1)
-    reg_copy.wait_recv()
-    own_k = (rk_s[:REG_DEV, :] + rrecv[0]) / divisor
-    own_v = (rv_s[:REG_DEV, :] + rrecv[1]) / divisor
-    for a in range(NA):
-        for b in range(NB):
-            mine = row8 == reg_ref[a, b]
-            rep = mrep[a, b * CELLS : (b + 1) * CELLS, :]
-            rep2 = jnp.concatenate([rep, rep], axis=1)
-            for own, total, out in ((own_k, dk_s, o_k), (own_v, dv_s, o_v)):
-                row = jnp.sum(jnp.where(mine, own, 0.0), axis=0, keepdims=True)
-                cells = total[a, b * CELLS : (b + 1) * CELLS, :] + rep2 * row
-                if b < 2:
-                    total[a, b * CELLS : (b + 1) * CELLS, :] = cells
-                else:
-                    out[a, :, b] = cells.reshape(WIN, WIN, 256).astype(BF16)
-
-    foreign_queries(0)
-    for a in range(NA):
-        for b in range(2):
-            for total, out in ((dk_s, o_k), (dv_s, o_v)):
-                cells = total[a, b * CELLS : (b + 1) * CELLS, :]
-                out[a, :, b] = cells.reshape(WIN, WIN, 256).astype(BF16)
+    foreign_keys(1)
+
+    def step(i, carry):
+        keys_now = i == jnp.where(first_tile, 2, 0)
+        number = jnp.where(first_tile & (i < 2), i + 1, i) - 1
+        side = jnp.where(first_tile, (i < 2).astype(jnp.int32), 1 - lax.rem(number + 4, 2))
+        a = jnp.where(first_tile, jnp.where(i < 2, i, i - 3), lax.div(number + 4, 2) - 2)
+
+        @pl.when(keys_now)
+        def _():
+            foreign_keys(0)
+            rsend[0] = rk_s[REG_DEV:, :]
+            rsend[1] = rv_s[REG_DEV:, :]
+            reg_copy.start()
+
+        @pl.when(jnp.logical_not(keys_now))
+        def _():
+            @pl.when(a == 0)
+            def _():
+                st_copy(1 - side).wait_recv()
+
+            foreign_queries(side, a)
+
+        @pl.when(jnp.logical_not(keys_now) & (side == 0) & (a == 0))
+        def _():
+            reg_copy.wait_recv()
+            rrecv[0] = (rk_s[:REG_DEV, :] + rrecv[0]) / divisor
+            rrecv[1] = (rv_s[:REG_DEV, :] + rrecv[1]) / divisor
+            spread(0, 0, NB)
+            spread(1, 2, 3)
+
+        @pl.when(i == 3)
+        def _():
+            spread(1, 3, NB)
+
+        return carry
+
+    lax.fori_loop(0, 5, step, 0)
+    spread(1, 0, 2)
     for side in range(2):
-        for copy in bulk(side) + [st_copy(side)]:
+        for copy in early(side) + later(side):
             copy.wait_send()
     pool_copy.wait_send()
     reg_copy.wait_send()
@@ -400,7 +443,7 @@
         + [dma((2, 2))] * 2
         + [dma((2, NA, 2))] * 2
         + [dma((2,))] * 6
-        + [pltpu.SemaphoreType.REGULAR],
+        + [pltpu.SemaphoreType.REGULAR] * 4,
         compiler_params=pltpu.CompilerParams(
             collective_id=0, has_side_effects=True, vmem_limit_bytes=VMEM_BYTES
         ),

time: 25.6 us -> 24.5 us (0.957)
  Pallas kernels: 24.8 us -> 23.7 us
    pallas_call x1, Pallas kernels: 23.9 us -> 22.7 us  [local(): pl.pallas_call(kernel, out_shape=[pltpu.VMEM(grid, BF16)] * 3, in_specs=[...]
where the time goes in v4:
time: 24.5 us; the launch traced here: 24.3 us
  Pallas kernels  23.7 us (97%)
  between operations  0.64 us (3%)
    pallas_call x1, Pallas kernels, local(): pl.pallas_call(kernel, out_shape=[pltpu.VMEM(grid, BF16)] * 3, in_specs=[...  22.7 us
    pallas_call x1, Pallas kernels, local(): pl.pallas_call(store, out_shape=[jax.ShapeDtypeStruct(grid, BF16)] * 3, i...  0.97 us

profile of v4, /device:TPU:1, one launch (start us, length us, event | category | flops | bytes accessed | tf_op | source)
XLA Modules:
  0.0 24.3 jit_solution(7114399556173633692)
XLA Ops:
  0.6 22.7 %shard_map.94 = (bf16[2,8,5,8,256]{4,3,2,1,0:T(8,128)(2,1)S(1)}, bf16[2,8,5,8,256]{4,3,2,1,0:T(8,128)(2,1)S(1)}, bf16[2,8,5,8,256]{4,3,2,1,0:T(8,128)(2,1)S(1)}) custom-call(bf16[2,8,5,8,256]{4,3,2,1,0:T(8,128)(2,1)} %bitcast.7, bf16[2,8,5,8,256]{4,3,2,1,0:T(8,128)(2,1)} %bitcast.8, bf16[2,8,5,8,256]{4,3,2,1,0:T(8,128)(2,1)} %bitcast.9, ...), custom_call_target="tpu_custom_call" | custom-call | flops 2200000000 | bytes 2300000 | tf_op jit(solution)/shard_map/pallas_call | solution.py:424
  23.4 1.0 %shard_map.95 = (bf16[2,8,5,8,256]{4,3,2,1,0:T(8,128)(2,1)}, bf16[2,8,5,8,256]{4,3,2,1,0:T(8,128)(2,1)}, bf16[2,8,5,8,256]{4,3,2,1,0:T(8,128)(2,1)}) custom-call(bf16[2,8,5,8,256]{4,3,2,1,0:T(8,128)(2,1)S(1)} %get-tuple-element.9.a_in, bf16[2,8,5,8,256]{4,3,2,1,0:T(8,128)(2,1)S(1)} %get-tuple-element.10.b_in, ...), custom_call_target="tpu_custom_call" | custom-call | tf_op jit(solution)/shard_map/pallas_call | solution.py:454

commit v5 on v4

--- a/solution.py
+++ b/solution.py
@@ -36,9 +36,9 @@
     o_q, o_k, o_v,
     q_in, k_in, v_in, g_in, kb, vb, mrep, frep,
     fk, fv, fq, fg, fmask, e_s, p_s, dk_s, dv_s, rk_s, rv_s,
-    pool, rsend, rrecv, st_out, st_in,
+    pool, rsend, rrecv, own_st, st_out, st_in, far_off,
     mask_ref, off_ref, reg_ref,
-    in_sem, kv_ss, kv_rs, qg_ss, qg_rs, mk_ss, mk_rs, st_ss, st_rs, lat_ss, lat_rs, late, go, chain, peer_in,
+    in_sem, kv_ss, kv_rs, qg_ss, qg_rs, mk_ss, mk_rs, st_ss, st_rs, of_ss, of_rs, one_ss, one_rs, lat_ss, lat_rs, late, go, chain, peer_in,
 ):
     count = lax.axis_size("lon")
     me = lax.axis_index("lon")
@@ -102,15 +102,25 @@
         dst = (fq, fg)[kind].at[1 - side, a]
         return remote(src, dst, qg_ss.at[side, a, kind], qg_rs.at[1 - side, a, kind], side)
 
+    def offset_copy(side):
+        return remote(off_hbm, far_off.at[1 - side], of_ss.at[side], of_rs.at[1 - side], side)
+
+    def one_copy(side, slot, kind):
+        src = (q_hbm, g_hbm)[kind].at[1, :, 3 * side + slot]
+        dst = (fq, fg)[kind].at[1 - side, 1, :, slot]
+        return remote(src, dst, one_ss.at[side, slot, kind], one_rs.at[1 - side, slot, kind], side)
+
     def st_copy(side):
         return remote(st_out.at[side], st_in.at[1 - side], st_ss.at[side], st_rs.at[1 - side], side)
 
     def early(side):
-        copies = [kv_copy(side, kind) for kind in range(2)] + [mask_copy(side)]
+        copies = [kv_copy(side, kind) for kind in range(2)] + [mask_copy(side), offset_copy(side)]
         return copies + [qg_copy(side, 0, kind) for kind in range(2)]
 
     def later(side):
-        return [st_copy(side)] + [qg_copy(side, 1, kind) for kind in range(2)]
+        outer = side
+        slots = (outer, 1 - outer)
+        return [st_copy(side)] + [one_copy(side, slot, kind) for slot in slots for kind in range(2)]
 
     for copy in early(1) + loads:
         copy.start()
@@ -146,6 +156,8 @@
 
     cell_t = lax.broadcasted_iota(jnp.int32, (CELLS, NB * WIN), 0) % WIN
     lane = lax.broadcasted_iota(jnp.int32, (CELLS, NB * WIN), 1)
+    off_row = lax.broadcasted_iota(jnp.int32, (NA, NB), 0)
+    off_col = lax.broadcasted_iota(jnp.int32, (NA, NB), 1)
     row8 = lax.broadcasted_iota(jnp.int32, (REG_DEV, 256), 0)
 
     def mask_rows(mask8):
@@ -264,8 +276,9 @@
             p_s[a, i, :rows] = dp
             slot = i % 2
             for r in range(3):
-                st_out[side, a, slot, r : r + 1] = stats[r]
-            st_out[side, a, slot, 3:4] = jnp.full((1, 256), off_ref[a, block], jnp.int32).astype(F32)
+                own_st[side, a, slot, r : r + 1] = stats[r]
+            st_out[side, a, slot, 0:1] = stats[0] + jnp.log(stats[1])
+            st_out[side, a, slot, 1:2] = stats[2] / stats[1]
         return carry
 
     def middle(a, carry):
@@ -300,7 +313,7 @@
                 bdq, bdg = local_q(a, block)
                 add = bias(frep[low * CELLS : high * CELLS, :], relative - block, off_ref[a, block])
                 far_e, far_dp, far = partial_stats(far_k, far_v, bdq, bdg, add)
-                near = tuple(st_out[side, a, i % 2, r : r + 1] for r in range(3))
+                near = tuple(own_st[side, a, i % 2, r : r + 1] for r in range(3))
                 alpha, far_alpha, delta = merged(near, far)
                 p, ds = weights(e_s[a, i, :rows], p_s[a, i, :rows], alpha, delta)
                 _, far_ds = weights(far_e, far_dp, far_alpha, delta)
@@ -311,23 +324,75 @@
 
         lax.fori_loop(0, NA, body, 0)
 
-    def foreign_queries(side, a):
+    def far_slot(side, blocks):
+        return blocks - 1 + side * (3 - 2 * blocks)
+
+    def row0_arrived(side):
+        offset_copy(1 - side).wait_recv()
+        st_copy(1 - side).wait_recv()
         for kind in range(2):
-            qg_copy(1 - side, a, kind).wait_recv()
-        for blocks in range(1, 3):
-            slot = blocks - 1 + side * (3 - 2 * blocks)
-            first = side * (NB - blocks)
-            relative = jnp.where(side == 0, blocks - 3, 7 - blocks)
-            cells = pl.ds(pl.multiple_of(first * CELLS, CELLS), blocks * CELLS)
-            bdq, bdg = diag_pair(fq[side, a, :, slot], fg[side, a, :, slot])
-            theirs = tuple(st_in[side, a, slot, r : r + 1] for r in range(3))
-            start = st_in[side, a, slot, 3:4, 0:128].astype(jnp.int32)
-            add = bias(mrep[a, cells, :], first - relative, start)
-            e, dp, stats = partial_stats(kb[a, cells, :], vb[a, cells, :], bdq, bdg, add)
-            alpha, _, delta = merged(stats, theirs)
-            p, ds = weights(e, dp, alpha, delta)
-            dv_s[a, cells, :] += dot(p, bdg)
-            dk_s[a, cells, :] += dot(ds, bdq)
+            qg_copy(1 - side, 0, kind).wait_recv()
+
+    def row1_arrived(side, blocks):
+        for kind in range(2):
+            one_copy(1 - side, far_slot(side, blocks), kind).wait_recv()
+
+    def far_weights(side, a, blocks):
+        slot = far_slot(side, blocks)
+        first = side * (NB - blocks)
+        relative = jnp.where(side == 0, blocks - 3, 7 - blocks)
+        cells = rows_of(first, blocks)
+        bdq, bdg = diag_pair(fq[side, a, :, slot], fg[side, a, :, slot])
+        top = st_in[side, a, slot, 0:1]
+        theirs = (top, jnp.ones_like(top), st_in[side, a, slot, 1:2])
+        here = (off_row == a) & (off_col == slot + 3 * (1 - side))
+        start = jnp.sum(
+            jnp.sum(jnp.where(here, far_off[side].astype(F32), 0.0), axis=1, keepdims=True),
+            axis=0, keepdims=True,
+        ).astype(jnp.int32)
+        add = bias(mrep[a, cells, :], first - relative, start)
+        e, dp, stats = partial_stats(kb[a, cells, :], vb[a, cells, :], bdq, bdg, add)
+        alpha, _, delta = merged(stats, theirs)
+        return cells, bdq, bdg, weights(e, dp, alpha, delta)
+
+    def add_far(a, unit):
+        cells, bdq, bdg, (p, ds) = unit
+        dv_s[a, cells, :] += dot(p, bdg)
+        dk_s[a, cells, :] += dot(ds, bdq)
+
+    def one_side(side, a):
+        @pl.when(a == 0)
+        def _():
+            row0_arrived(side)
+
+        for blocks in (2, 1):
+            @pl.when(a == 1)
+            def _():
+                row1_arrived(side, blocks)
+
+            add_far(a, far_weights(side, a, blocks))
+
+    def both_sides(a):
+        @pl.when(a == 0)
+        def _():
+            for side in range(2):
+                row0_arrived(side)
+
+        @pl.when(a == 1)
+        def _():
+            for side in range(2):
+                for blocks in (2, 1):
+                    row1_arrived(side, blocks)
+
+        units = [far_weights(side, a, blocks) for blocks in (2, 1) for side in range(2)]
+        for unit in units:
+            add_far(a, unit)
+
+    def rows_of(first, blocks):
+        start = first * CELLS
+        if not isinstance(start, int):
+            start = pl.multiple_of(start, CELLS)
+        return pl.ds(start, blocks * CELLS)
 
     def spread(a, low, high):
         for b in range(low, high):
@@ -361,42 +426,43 @@
     )
     foreign_keys(1)
 
+    def left_keys():
+        foreign_keys(0)
+        rsend[0] = rk_s[REG_DEV:, :]
+        rsend[1] = rv_s[REG_DEV:, :]
+        reg_copy.start()
+
+    def registers_done():
+        reg_copy.wait_recv()
+        rrecv[0] = (rk_s[:REG_DEV, :] + rrecv[0]) / divisor
+        rrecv[1] = (rv_s[:REG_DEV, :] + rrecv[1]) / divisor
+
     def step(i, carry):
-        keys_now = i == jnp.where(first_tile, 2, 0)
-        number = jnp.where(first_tile & (i < 2), i + 1, i) - 1
-        side = jnp.where(first_tile, (i < 2).astype(jnp.int32), 1 - lax.rem(number + 4, 2))
-        a = jnp.where(first_tile, jnp.where(i < 2, i, i - 3), lax.div(number + 4, 2) - 2)
-
-        @pl.when(keys_now)
-        def _():
-            foreign_keys(0)
-            rsend[0] = rk_s[REG_DEV:, :]
-            rsend[1] = rv_s[REG_DEV:, :]
-            reg_copy.start()
-
-        @pl.when(jnp.logical_not(keys_now))
-        def _():
-            @pl.when(a == 0)
-            def _():
-                st_copy(1 - side).wait_recv()
-
-            foreign_queries(side, a)
-
-        @pl.when(jnp.logical_not(keys_now) & (side == 0) & (a == 0))
-        def _():
-            reg_copy.wait_recv()
-            rrecv[0] = (rk_s[:REG_DEV, :] + rrecv[0]) / divisor
-            rrecv[1] = (rv_s[:REG_DEV, :] + rrecv[1]) / divisor
+        @pl.when(i == jnp.where(first_tile, 2, 0))
+        def _():
+            left_keys()
+
+        @pl.when(first_tile & (i != 2))
+        def _():
+            one_side((i < 2).astype(jnp.int32), jnp.where(i < 2, i, i - 3))
+
+        @pl.when(jnp.logical_not(first_tile) & (i > 0))
+        def _():
+            both_sides(i - 1)
+
+        @pl.when(i == jnp.where(first_tile, 3, 1))
+        def _():
+            registers_done()
             spread(0, 0, NB)
             spread(1, 2, 3)
 
-        @pl.when(i == 3)
+        @pl.when(i == jnp.where(first_tile, 3, 2))
         def _():
             spread(1, 3, NB)
 
         return carry
 
-    lax.fori_loop(0, 5, step, 0)
+    lax.fori_loop(0, jnp.where(first_tile, 5, 3), step, 0)
     spread(1, 0, 2)
     for side in range(2):
         for copy in early(side) + later(side):
@@ -436,13 +502,17 @@
         + [vm((2 * REG_DEV, 256), F32)] * 2
         + [vm((2, 2, REG_DEV, 256), BF16)]
         + [vm((2, REG_DEV, 256), F32)] * 2
-        + [vm((2, NA, 2, 8, 256), F32)] * 2
+        + [vm((2, NA, 2, 8, 256), F32)]
+        + [vm((2, NA, 2, 2, 256), F32)] * 2
+        + [vm((2,) + offsets.shape, jnp.int32)]
         + [vm(key_mask.shape, jnp.int32)]
         + [pltpu.SMEM(offsets.shape, jnp.int32)] * 2
         + [dma((7,))]
         + [dma((2, 2))] * 2
         + [dma((2, NA, 2))] * 2
         + [dma((2,))] * 6
+        + [dma((2, 2, 2))] * 2
+        + [dma((2,))] * 2
         + [pltpu.SemaphoreType.REGULAR] * 4,
         compiler_params=pltpu.CompilerParams(
             collective_id=0, has_side_effects=True, vmem_limit_bytes=VMEM_BYTES

time: 24.5 us -> 23.9 us (0.976)
  Pallas kernels: 23.7 us -> 23.1 us
    pallas_call x1, Pallas kernels: 22.7 us -> 22.1 us  [local(): pl.pallas_call(kernel, out_shape=[pltpu.VMEM(grid, BF16)] * 3, in_specs=[...]
where the time goes in v5:
time: 23.9 us; the launch traced here: 23.7 us
  Pallas kernels  23.1 us (97%)
  between operations  0.64 us (3%)
    pallas_call x1, Pallas kernels, local(): pl.pallas_call(kernel, out_shape=[pltpu.VMEM(grid, BF16)] * 3, in_specs=[...  22.1 us
    pallas_call x1, Pallas kernels, local(): pl.pallas_call(store, out_shape=[jax.ShapeDtypeStruct(grid, BF16)] * 3, i...  0.97 us

profile of v5, /device:TPU:1, one launch (start us, length us, event | category | flops | bytes accessed | tf_op | source)
XLA Modules:
  0.0 23.7 jit_solution(3119860154115438054)
XLA Ops:
  0.6 22.1 %shard_map.94 = (bf16[2,8,5,8,256]{4,3,2,1,0:T(8,128)(2,1)S(1)}, bf16[2,8,5,8,256]{4,3,2,1,0:T(8,128)(2,1)S(1)}, bf16[2,8,5,8,256]{4,3,2,1,0:T(8,128)(2,1)S(1)}) custom-call(bf16[2,8,5,8,256]{4,3,2,1,0:T(8,128)(2,1)} %bitcast.7, bf16[2,8,5,8,256]{4,3,2,1,0:T(8,128)(2,1)} %bitcast.8, bf16[2,8,5,8,256]{4,3,2,1,0:T(8,128)(2,1)} %bitcast.9, ...), custom_call_target="tpu_custom_call" | custom-call | flops 2200000000 | bytes 2300000 | tf_op jit(solution)/shard_map/pallas_call | solution.py:490
  22.7 1.0 %shard_map.95 = (bf16[2,8,5,8,256]{4,3,2,1,0:T(8,128)(2,1)}, bf16[2,8,5,8,256]{4,3,2,1,0:T(8,128)(2,1)}, bf16[2,8,5,8,256]{4,3,2,1,0:T(8,128)(2,1)}) custom-call(bf16[2,8,5,8,256]{4,3,2,1,0:T(8,128)(2,1)S(1)} %get-tuple-element.9.a_in, bf16[2,8,5,8,256]{4,3,2,1,0:T(8,128)(2,1)S(1)} %get-tuple-element.10.b_in, ...), custom_call_target="tpu_custom_call" | custom-call | tf_op jit(solution)/shard_map/pallas_call | solution.py:524

commit v6 on v5

--- a/solution.py
+++ b/solution.py
@@ -220,21 +220,28 @@
         dp = dot(values, bdg, NT)
         top = jnp.maximum(jnp.max(s, axis=0, keepdims=True), FLOOR)
         e = jnp.exp(s - top)
-        total = jnp.sum(e, axis=0, keepdims=True)
-        inner = jnp.sum(e * dp, axis=0, keepdims=True)
-        return e, dp, (top, total, inner)
+        return e, dp, (top, jnp.sum(e, axis=0, keepdims=True))
 
     def merged(x, y):
         top = jnp.maximum(x[0], y[0])
         fx = jnp.exp(x[0] - top)
         fy = jnp.exp(y[0] - top)
         inverse = 1.0 / (x[1] * fx + y[1] * fy)
-        return fx * inverse, fy * inverse, (x[2] * fx + y[2] * fy) * inverse
-
-    def weights(e, dp, alpha, delta):
+        return fx * inverse, fy * inverse
+
+    def probabilities(e, dp, alpha):
         p = e * alpha
-        ds = p * (dp - delta)
-        return p.astype(BF16), ds.astype(BF16)
+        low = p.astype(BF16)
+        return p, low, jnp.sum(low.astype(F32) * dp, axis=0, keepdims=True)
+
+    def score_grads(p, dp, delta):
+        return (p * (dp - delta)).astype(BF16)
+
+    def rows_of(first, blocks):
+        start = first * CELLS
+        if not isinstance(start, int):
+            start = pl.multiple_of(start, CELLS)
+        return pl.ds(start, blocks * CELLS)
 
     def add_key_grads(a, first, end, p, ds, bdq, bdg, regs):
         rows = (end - first) * CELLS
@@ -275,17 +282,17 @@
             e_s[a, i, :rows] = e
             p_s[a, i, :rows] = dp
             slot = i % 2
-            for r in range(3):
+            for r in range(2):
                 own_st[side, a, slot, r : r + 1] = stats[r]
             st_out[side, a, slot, 0:1] = stats[0] + jnp.log(stats[1])
-            st_out[side, a, slot, 1:2] = stats[2] / stats[1]
+            st_out[side, a, slot, 1:2] = probabilities(e, dp, 1.0 / stats[1])[2]
         return carry
 
     def middle(a, carry):
         keys, bdq, bdg, e, dp, stats = local_stats(a, 2, 0, NB)
-        inverse = 1.0 / stats[1]
-        p, ds = weights(e, dp, inverse, stats[2] * inverse)
-        add_key_grads(a, 0, NB, p, ds, bdq, bdg, True)
+        p, low, delta = probabilities(e, dp, 1.0 / stats[1])
+        ds = score_grads(p, dp, delta)
+        add_key_grads(a, 0, NB, low, ds, bdq, bdg, True)
         dq = diag_rows(dot(ds, keys, TN)) * SCALE
         o_q[a, :, 2] = dq.reshape(WIN, WIN, 256).astype(BF16)
         return carry
@@ -313,12 +320,16 @@
                 bdq, bdg = local_q(a, block)
                 add = bias(frep[low * CELLS : high * CELLS, :], relative - block, off_ref[a, block])
                 far_e, far_dp, far = partial_stats(far_k, far_v, bdq, bdg, add)
-                near = tuple(own_st[side, a, i % 2, r : r + 1] for r in range(3))
-                alpha, far_alpha, delta = merged(near, far)
-                p, ds = weights(e_s[a, i, :rows], p_s[a, i, :rows], alpha, delta)
-                _, far_ds = weights(far_e, far_dp, far_alpha, delta)
+                near = tuple(own_st[side, a, i % 2, r : r + 1] for r in range(2))
+                alpha, far_alpha = merged(near, far)
+                dp = p_s[a, i, :rows]
+                p, low_p, share = probabilities(e_s[a, i, :rows], dp, alpha)
+                far_p, _, far_share = probabilities(far_e, far_dp, far_alpha)
+                delta = share + far_share
+                ds = score_grads(p, dp, delta)
+                far_ds = score_grads(far_p, far_dp, delta)
                 dq = diag_rows(dot(ds, keys, TN) + dot(far_ds, far_k, TN)) * SCALE
-                add_key_grads(a, first, end, p, ds, bdq, bdg, True)
+                add_key_grads(a, first, end, low_p, ds, bdq, bdg, True)
                 o_q[a, :, block] = dq.reshape(WIN, WIN, 256).astype(BF16)
             return carry
 
@@ -344,7 +355,7 @@
         cells = rows_of(first, blocks)
         bdq, bdg = diag_pair(fq[side, a, :, slot], fg[side, a, :, slot])
         top = st_in[side, a, slot, 0:1]
-        theirs = (top, jnp.ones_like(top), st_in[side, a, slot, 1:2])
+        theirs = (top, jnp.ones_like(top))
         here = (off_row == a) & (off_col == slot + 3 * (1 - side))
         start = jnp.sum(
             jnp.sum(jnp.where(here, far_off[side].astype(F32), 0.0), axis=1, keepdims=True),
@@ -352,8 +363,10 @@
         ).astype(jnp.int32)
         add = bias(mrep[a, cells, :], first - relative, start)
         e, dp, stats = partial_stats(kb[a, cells, :], vb[a, cells, :], bdq, bdg, add)
-        alpha, _, delta = merged(stats, theirs)
-        return cells, bdq, bdg, weights(e, dp, alpha, delta)
+        alpha, their_alpha = merged(stats, theirs)
+        p, low, share = probabilities(e, dp, alpha)
+        ds = score_grads(p, dp, share + their_alpha * st_in[side, a, slot, 1:2])
+        return cells, bdq, bdg, (low, ds)
 
     def add_far(a, unit):
         cells, bdq, bdg, (p, ds) = unit
@@ -387,12 +400,6 @@
         units = [far_weights(side, a, blocks) for blocks in (2, 1) for side in range(2)]
         for unit in units:
             add_far(a, unit)
-
-    def rows_of(first, blocks):
-        start = first * CELLS
-        if not isinstance(start, int):
-            start = pl.multiple_of(start, CELLS)
-        return pl.ds(start, blocks * CELLS)
 
     def spread(a, low, high):
         for b in range(low, high):

time: 23.9 us -> 23.9 us (level)
  no operation moved by 1% of the time
where the time goes in v6:
time: 23.9 us; the launch traced here: 23.7 us
  Pallas kernels  23.1 us (97%)
  between operations  0.64 us (3%)
    pallas_call x1, Pallas kernels, local(): pl.pallas_call(kernel, out_shape=[pltpu.VMEM(grid, BF16)] * 3, in_specs=[...  22.1 us
    pallas_call x1, Pallas kernels, local(): pl.pallas_call(store, out_shape=[jax.ShapeDtypeStruct(grid, BF16)] * 3, i...  0.97 us

profile of v6, /device:TPU:1, one launch (start us, length us, event | category | flops | bytes accessed | tf_op | source)
XLA Modules:
  0.0 23.7 jit_solution(12828201158299422370)
XLA Ops:
  0.6 22.1 %shard_map.94 = (bf16[2,8,5,8,256]{4,3,2,1,0:T(8,128)(2,1)S(1)}, bf16[2,8,5,8,256]{4,3,2,1,0:T(8,128)(2,1)S(1)}, bf16[2,8,5,8,256]{4,3,2,1,0:T(8,128)(2,1)S(1)}) custom-call(bf16[2,8,5,8,256]{4,3,2,1,0:T(8,128)(2,1)} %bitcast.7, bf16[2,8,5,8,256]{4,3,2,1,0:T(8,128)(2,1)} %bitcast.8, bf16[2,8,5,8,256]{4,3,2,1,0:T(8,128)(2,1)} %bitcast.9, ...), custom_call_target="tpu_custom_call" | custom-call | flops 2200000000 | bytes 2300000 | tf_op jit(solution)/shard_map/pallas_call | solution.py:497
  22.8 1.0 %shard_map.95 = (bf16[2,8,5,8,256]{4,3,2,1,0:T(8,128)(2,1)}, bf16[2,8,5,8,256]{4,3,2,1,0:T(8,128)(2,1)}, bf16[2,8,5,8,256]{4,3,2,1,0:T(8,128)(2,1)}) custom-call(bf16[2,8,5,8,256]{4,3,2,1,0:T(8,128)(2,1)S(1)} %get-tuple-element.9.a_in, bf16[2,8,5,8,256]{4,3,2,1,0:T(8,128)(2,1)S(1)} %get-tuple-element.10.b_in, ...), custom_call_target="tpu_custom_call" | custom-call | tf_op jit(solution)/shard_map/pallas_call | solution.py:531

commit v7 on v6

--- a/solution.py
+++ b/solution.py
@@ -469,7 +469,16 @@
 
         return carry
 
-    lax.fori_loop(0, jnp.where(first_tile, 5, 3), step, 0)
+    lax.fori_loop(0, jnp.where(first_tile, 4, 3), step, 0)
+
+    @pl.when(first_tile)
+    def _():
+        for blocks in (2, 1):
+            row1_arrived(0, blocks)
+        units = [far_weights(0, 1, blocks) for blocks in (2, 1)]
+        for unit in units:
+            add_far(1, unit)
+
     spread(1, 0, 2)
     for side in range(2):
         for copy in early(side) + later(side):

time: 23.9 us -> 24 us (level)
  no operation moved by 1% of the time
where the time goes in v7:
time: 24 us; the launch traced here: 23.8 us
  Pallas kernels  23.2 us (97%)
  between operations  0.64 us (3%)
    pallas_call x1, Pallas kernels, local(): pl.pallas_call(kernel, out_shape=[pltpu.VMEM(grid, BF16)] * 3, in_specs=[...  22.2 us
    pallas_call x1, Pallas kernels, local(): pl.pallas_call(store, out_shape=[jax.ShapeDtypeStruct(grid, BF16)] * 3, i...  0.97 us

profile of v7, /device:TPU:1, one launch (start us, length us, event | category | flops | bytes accessed | tf_op | source)
XLA Modules:
  0.0 23.8 jit_solution(13735846178138539031)
XLA Ops:
  0.6 22.2 %shard_map.94 = (bf16[2,8,5,8,256]{4,3,2,1,0:T(8,128)(2,1)S(1)}, bf16[2,8,5,8,256]{4,3,2,1,0:T(8,128)(2,1)S(1)}, bf16[2,8,5,8,256]{4,3,2,1,0:T(8,128)(2,1)S(1)}) custom-call(bf16[2,8,5,8,256]{4,3,2,1,0:T(8,128)(2,1)} %bitcast.7, bf16[2,8,5,8,256]{4,3,2,1,0:T(8,128)(2,1)} %bitcast.8, bf16[2,8,5,8,256]{4,3,2,1,0:T(8,128)(2,1)} %bitcast.9, ...), custom_call_target="tpu_custom_call" | custom-call | flops 2200000000 | bytes 2300000 | tf_op jit(solution)/shard_map/pallas_call | solution.py:506
  22.8 1.0 %shard_map.95 = (bf16[2,8,5,8,256]{4,3,2,1,0:T(8,128)(2,1)}, bf16[2,8,5,8,256]{4,3,2,1,0:T(8,128)(2,1)}, bf16[2,8,5,8,256]{4,3,2,1,0:T(8,128)(2,1)}) custom-call(bf16[2,8,5,8,256]{4,3,2,1,0:T(8,128)(2,1)S(1)} %get-tuple-element.9.a_in, bf16[2,8,5,8,256]{4,3,2,1,0:T(8,128)(2,1)S(1)} %get-tuple-element.10.b_in, ...), custom_call_target="tpu_custom_call" | custom-call | tf_op jit(solution)/shard_map/pallas_call | solution.py:540

commit v8 on v7

--- a/solution.py
+++ b/solution.py
@@ -348,7 +348,19 @@
         for kind in range(2):
             one_copy(1 - side, far_slot(side, blocks), kind).wait_recv()
 
-    def far_weights(side, a, blocks):
+    def far_bias(side, a, blocks):
+        slot = far_slot(side, blocks)
+        first = side * (NB - blocks)
+        relative = jnp.where(side == 0, blocks - 3, 7 - blocks)
+        cells = rows_of(first, blocks)
+        here = (off_row == a) & (off_col == slot + 3 * (1 - side))
+        start = jnp.sum(
+            jnp.sum(jnp.where(here, far_off[side].astype(F32), 0.0), axis=1, keepdims=True),
+            axis=0, keepdims=True,
+        ).astype(jnp.int32)
+        return bias(mrep[a, cells, :], first - relative, start)
+
+    def far_weights(side, a, blocks, add=None):
         slot = far_slot(side, blocks)
         first = side * (NB - blocks)
         relative = jnp.where(side == 0, blocks - 3, 7 - blocks)
@@ -356,12 +368,8 @@
         bdq, bdg = diag_pair(fq[side, a, :, slot], fg[side, a, :, slot])
         top = st_in[side, a, slot, 0:1]
         theirs = (top, jnp.ones_like(top))
-        here = (off_row == a) & (off_col == slot + 3 * (1 - side))
-        start = jnp.sum(
-            jnp.sum(jnp.where(here, far_off[side].astype(F32), 0.0), axis=1, keepdims=True),
-            axis=0, keepdims=True,
-        ).astype(jnp.int32)
-        add = bias(mrep[a, cells, :], first - relative, start)
+        if add is None:
+            add = far_bias(side, a, blocks)
         e, dp, stats = partial_stats(kb[a, cells, :], vb[a, cells, :], bdq, bdg, add)
         alpha, their_alpha = merged(stats, theirs)
         p, low, share = probabilities(e, dp, alpha)
@@ -473,9 +481,10 @@
 
     @pl.when(first_tile)
     def _():
+        adds = {blocks: far_bias(0, 1, blocks) for blocks in (2, 1)}
         for blocks in (2, 1):
             row1_arrived(0, blocks)
-        units = [far_weights(0, 1, blocks) for blocks in (2, 1)]
+        units = [far_weights(0, 1, blocks, adds[blocks]) for blocks in (2, 1)]
         for unit in units:
             add_far(1, unit)
 

time: 24 us -> 24 us (level)
  no operation moved by 1% of the time
where the time goes in v8:
time: 24 us; the launch traced here: 23.8 us
  Pallas kernels  23.2 us (97%)
  between operations  0.64 us (3%)
    pallas_call x1, Pallas kernels, local(): pl.pallas_call(kernel, out_shape=[pltpu.VMEM(grid, BF16)] * 3, in_specs=[...  22.2 us
    pallas_call x1, Pallas kernels, local(): pl.pallas_call(store, out_shape=[jax.ShapeDtypeStruct(grid, BF16)] * 3, i...  0.97 us

profile of v8, /device:TPU:1, one launch (start us, length us, event | category | flops | bytes accessed | tf_op | source)
XLA Modules:
  0.0 23.8 jit_solution(56099498425039442)
XLA Ops:
  0.6 22.2 %shard_map.94 = (bf16[2,8,5,8,256]{4,3,2,1,0:T(8,128)(2,1)S(1)}, bf16[2,8,5,8,256]{4,3,2,1,0:T(8,128)(2,1)S(1)}, bf16[2,8,5,8,256]{4,3,2,1,0:T(8,128)(2,1)S(1)}) custom-call(bf16[2,8,5,8,256]{4,3,2,1,0:T(8,128)(2,1)} %bitcast.7, bf16[2,8,5,8,256]{4,3,2,1,0:T(8,128)(2,1)} %bitcast.8, bf16[2,8,5,8,256]{4,3,2,1,0:T(8,128)(2,1)} %bitcast.9, ...), custom_call_target="tpu_custom_call" | custom-call | flops 2200000000 | bytes 2300000 | tf_op jit(solution)/shard_map/pallas_call | solution.py:515
  22.8 1.0 %shard_map.95 = (bf16[2,8,5,8,256]{4,3,2,1,0:T(8,128)(2,1)}, bf16[2,8,5,8,256]{4,3,2,1,0:T(8,128)(2,1)}, bf16[2,8,5,8,256]{4,3,2,1,0:T(8,128)(2,1)}) custom-call(bf16[2,8,5,8,256]{4,3,2,1,0:T(8,128)(2,1)S(1)} %get-tuple-element.9.a_in, bf16[2,8,5,8,256]{4,3,2,1,0:T(8,128)(2,1)S(1)} %get-tuple-element.10.b_in, ...), custom_call_target="tpu_custom_call" | custom-call | tf_op jit(solution)/shard_map/pallas_call | solution.py:549
